TPU v7x, 256 devices: a whole 4x4x8 slice. The times are simulated.
256 devices in a mesh: dp: 32 (over z_lo, x, y), tensor: 8 (over z_hi, core).
Axes of the slice: x: 4, y: 4, z: 8 (z_hi: 4, z_lo: 2; z = z_hi * 2 + z_lo), core: 2. Of those that a mesh axis runs over, the one named last changes fastest.
Arguments:
- teacher_hidden: bfloat16 [32768, 6400], P('dp', 'tensor'), may hold values from -6 to 6
- down_weight: bfloat16 [6400, 3200], P('tensor'), may hold values from -0.109375 to 0.109375
- teacher_resid: bfloat16 [32768, 3200], P('dp', 'tensor'), may hold values from -6 to 6
- layer_scale: float32 [3200], replicated, may hold values from 0.3 to 3
- student_x: bfloat16 [32768, 1024], P(('dp', 'tensor')), may hold values from -0.3125 to 0.3125
- norm_gain: float32 [1024], replicated, may hold values from 0.5 to 1.5
- head_weight: bfloat16 [1024, 3200], P(None, 'tensor'), may hold values from -0.1875 to 0.1875
Outputs:
- token_loss: float32 [32768], P(('dp', 'tensor'))
- input_grad: bfloat16 [32768, 1024], P(('dp', 'tensor'))
- head_grad: bfloat16 [1024, 3200], P('dp', 'tensor')
All inputs are finite; a program needn't handle non-finite values.
Results may differ from a plain program's by a relative error of at most 0.02.
Values may be sent and summed in bfloat16 or wider, within the bound.
A program may use at most 128 MiB of HBM per device.

v0:
```python
import jax
import jax.numpy as jnp
from jax import lax
from jax.sharding import PartitionSpec as P

epsilon = 1e-06


def normalize(student_x, norm_gain):
    values = student_x.astype(jnp.float32)
    centered = values - jnp.mean(values, axis=1, keepdims=True)
    inverse = lax.rsqrt(jnp.mean(centered * centered, axis=1, keepdims=True) + epsilon)
    normed = centered * inverse
    normed_out = (normed * norm_gain).astype(jnp.bfloat16)
    return (normed, inverse, normed_out)


def norm_backward(back_grad, normed, inverse, norm_gain):
    normed_grad = back_grad * norm_gain
    return inverse * (
        normed_grad
        - jnp.mean(normed_grad, axis=1, keepdims=True)
        - normed * jnp.mean(normed_grad * normed, axis=1, keepdims=True)
    )


def cosine_parts(predicted, target_wide, inner_sum, pred_sq, target_sq):
    scaling = lax.rsqrt((pred_sq + epsilon) * (target_sq + epsilon))
    cosine = inner_sum * scaling
    pred_grad = (
        (cosine / (pred_sq + epsilon))[:, None] * predicted - scaling[:, None] * target_wide
    ).astype(jnp.bfloat16)
    return (1.0 - cosine, pred_grad)


def teacher_columns(teacher_hidden, down_weight, teacher_resid, layer_scale):
    column_count = teacher_resid.shape[1]
    first_column = lax.axis_index("tensor") * column_count
    partial_sum = jnp.dot(teacher_hidden, down_weight, preferred_element_type=jnp.float32)
    summed = lax.psum_scatter(
        partial_sum.astype(jnp.bfloat16), "tensor", scatter_dimension=1, tiled=True
    ).astype(jnp.float32)
    scale_part = lax.dynamic_slice_in_dim(layer_scale, first_column, column_count)
    return (teacher_resid.astype(jnp.float32) + scale_part * summed).astype(jnp.bfloat16)


def shards(
    teacher_hidden, down_weight, teacher_resid, layer_scale, student_x, norm_gain, head_weight
):
    normed, inverse, normed_out = normalize(student_x, norm_gain)
    feature_block = teacher_columns(teacher_hidden, down_weight, teacher_resid, layer_scale)
    target = lax.all_to_all(feature_block, "tensor", split_axis=0, concat_axis=1, tiled=True)
    full_head = lax.all_gather(head_weight, "tensor", axis=1, tiled=True)
    predicted = jnp.dot(normed_out, full_head, preferred_element_type=jnp.float32)
    target_wide = target.astype(jnp.float32)
    losses, pred_grad = cosine_parts(
        predicted,
        target_wide,
        jnp.sum(predicted * target_wide, axis=1),
        jnp.sum(predicted * predicted, axis=1),
        jnp.sum(target_wide * target_wide, axis=1),
    )
    grad_full = lax.dot_general(
        normed_out, pred_grad, (((0,), (0,)), ((), ())), preferred_element_type=jnp.float32
    )
    grad_block = lax.psum_scatter(grad_full, "tensor", scatter_dimension=1, tiled=True)
    back_grad = lax.dot_general(
        pred_grad, full_head, (((1,), (1,)), ((), ())), preferred_element_type=jnp.float32
    )
    head_grad = lax.psum_scatter(grad_block, "dp", scatter_dimension=0, tiled=True).astype(
        jnp.bfloat16
    )
    input_grad = norm_backward(back_grad, normed, inverse, norm_gain).astype(jnp.bfloat16)
    return (losses, input_grad, head_grad)


def solution(mesh):
    placed = (
        P("dp", "tensor"),
        P("tensor", None),
        P("dp", "tensor"),
        P(),
        P(("dp", "tensor"), None),
        P(),
        P(None, "tensor"),
    )
    return jax.shard_map(
        shards,
        mesh=mesh,
        in_specs=placed,
        out_specs=(P(("dp", "tensor")), P(("dp", "tensor"), None), P("dp", "tensor")),
        check_vma=False,
    )
```

profile of v0, /device:TPU:64, one launch (start us, length us, event | category | flops | bytes accessed | tf_op | source)
XLA Modules:
  0.0 516.1 jit_solution(10980891424135444829)
XLA Ops:
  7.2 0.0 reduce-scatter.6.cloned.1.call-start
  7.2 1.4 copy-done
  8.6 11.5 %convolution_convert_fusion = bf16[1024,3200]{0,1:T(8,128)(2,1)} fusion(bf16[1024,800]{0,1:T(8,128)(2,1)S(1)} %copy-done, bf16[800,3200]{1,0:T(8,128)(2,1)} %param.8), kind=kOutput, calls=%fused_computation | convolution fusion | flops 5246156800 | bytes 13312000 | tf_op jit(solution)/shard_map/dot_general | solution.py:39
  20.1 0.0 all-gather.2.cloned.1.call-start
  20.2 0.7 all-gather.2.cloned.1.call-update
  20.9 0.8 dynamic_slice.3
  21.7 78.8 %reduce-scatter.6.cloned.1.call-done = bf16[1024,400]{0,1:T(8,128)(2,1)} async-done(((bf16[1024,3200]{0,1:T(8,128)(2,1)}), bf16[1024,400]{0,1:T(8,128)(2,1)}) %reduce-scatter.6.cloned.1.call-update) | async-done | bytes 819216 | tf_op jit(solution)/shard_map/reduce_scatter | solution.py:40
  100.5 2.4 copy_bitcast_fusion
  102.9 7.1 %all-to-all-start = ((bf16[8,128,400]{1,2,0:T(8,128)(2,1)}), bf16[8,128,400]{1,2,0:T(8,128)(2,1)S(1)}, u32[]{:S(2)}, u32[]{:S(2)}) async-start(bf16[8,128,400]{1,2,0:T(8,128)(2,1)} %copy_bitcast_fusion), calls=%async_computation.1 | async-start | bytes 1638400 | tf_op jit(solution)/shard_map/all_to_all | solution.py:52
  110.0 0.1 convert_reduce_fusion
  110.1 0.2 fusion.11
  110.4 50.1 %all-to-all-done = bf16[8,128,400]{1,2,0:T(8,128)(2,1)S(1)} async-done(((bf16[8,128,400]{1,2,0:T(8,128)(2,1)}), bf16[8,128,400]{1,2,0:T(8,128)(2,1)S(1)}, u32[]{:S(2)}, u32[]{:S(2)}) %all-to-all-start) | async-done | bytes 819232 | tf_op jit(solution)/shard_map/all_to_all | solution.py:52
  160.4 1.4 convert_element_type.54
  161.8 0.1 copy-done.4
  161.9 1.9 copy.17
  163.8 2.1 multiply_reduce_fusion
  165.9 19.8 %all-gather.2.cloned.1.call-done = bf16[1024,3200]{0,1:T(8,128)(2,1)} async-done(((bf16[1024,400]{0,1:T(8,128)(2,1)}), bf16[1024,3200]{0,1:T(8,128)(2,1)}) %all-gather.2.cloned.1.call-update) | async-done | bytes 6553616 | tf_op jit(solution)/shard_map/all_gather | solution.py:53
  185.8 5.2 %multiply_reduce_fusion.1 = (f32[128]{0:T(128)S(1)}, f32[128]{0:T(128)S(1)}, f32[128,3200]{1,0:T(8,128)S(1)}) fusion(f32[128,3200]{1,0:T(8,128)S(1)} %copy.17, bf16[1024,3200]{0,1:T(8,128)(2,1)} %all-gather.2.cloned.1.call-done, bf16[128,1024]{1,0:T(8,128)(2,1)S(1)} %copy-done.3, f32[1024]{0:T(1024)S(1)} %copy-done.6, f32[128]{0:T(128)S(1)} %add_rsqrt_fusion, ...), kind=kOutput, calls=%fused_computation.3 | convolution fusion | flops 841154304 | bytes 10098688 | tf_op jit(solution)/shard_map/dot_general | solution.py:54
  191.0 0.3 subtract_convert_fusion
  191.4 0.2 copy-done.7
  191.6 0.9 copy-done.1
  192.5 6.6 %fusion.12 = f32[1024,3200]{0,1:T(8,128)} fusion(bf16[128,3200]{1,0:T(8,128)(2,1)S(1)} %subtract_convert_fusion, bf16[128,1024]{1,0:T(8,128)(2,1)S(1)} %copy-done.3, f32[1024]{0:T(1024)S(1)} %copy-done.6, f32[128]{0:T(128)S(1)} %add_rsqrt_fusion, f32[128]{0:T(128)S(1)} %broadcast_multiply_fusion.2), kind=kOutput, calls=%fused_computation.29 | convolution fusion | flops 839516160 | bytes 14193664 | tf_op jit(solution)/shard_map/dot_general | solution.py:63
  199.1 0.0 reduce-scatter.10.cloned.1.call-start
  199.2 138.0 %reduce-scatter.8.cloned.1.call-done = f32[1024,400]{0,1:T(8,128)} async-done(((f32[1024,3200]{0,1:T(8,128)}), f32[1024,400]{0,1:T(8,128)}) %reduce-scatter.8.cloned.1.call-update) | async-done | bytes 1638416 | tf_op jit(solution)/shard_map/reduce_scatter | solution.py:66
  337.1 2.9 copy.20
  340.0 0.6 copy-done.8
  340.7 0.5 broadcast_subtract_fusion
  341.2 4.1 fusion.16
  345.3 0.9 fusion.10
  346.2 161.7 %reduce-scatter.10.cloned.1.call-done = f32[32,400]{1,0:T(8,128)} async-done(((f32[1024,400]{1,0:T(8,128)}), f32[32,400]{1,0:T(8,128)}) %reduce-scatter.10.cloned.1.call-update) | async-done | bytes 51216
  507.9 1.0 copy.21
  508.8 0.7 copy.19
  (23 shorter events, 0.1 us)
Async XLA Ops:
  7.2 1.4 copy-start
  7.2 93.3 %reduce-scatter.6.cloned.1.call-start = ((), (), s32[]{:S(2)}) async-start(), calls=%async_computation.5 | async-start | bytes 7372800 | tf_op jit(solution)/shard_map/reduce_scatter | solution.py:40
  20.1 80.4 %copy-start.5 = (bf16[1024,400]{0,1:T(8,128)(2,1)S(1)}, bf16[1024,400]{0,1:T(8,128)(2,1)}, u32[]{:S(2)}) copy-start(bf16[1024,400]{0,1:T(8,128)(2,1)} %param.9) | copy-start | bytes 2457604
  20.1 165.6 %all-gather.2.cloned.1.call-start = ((), (), s32[]{:S(2)}) async-start(), calls=%async_computation.4 | async-start | bytes 7372800 | tf_op jit(solution)/shard_map/all_gather | solution.py:53
  21.7 88.3 %copy-start.3 = (bf16[128,1024]{1,0:T(8,128)(2,1)S(1)}, bf16[128,1024]{1,0:T(8,128)(2,1)}, u32[]{:S(2)}) copy-start(bf16[128,1024]{1,0:T(8,128)(2,1)} %param.11) | copy-start | bytes 786436
  102.9 57.6 %all-to-all-start = ((bf16[8,128,400]{1,2,0:T(8,128)(2,1)}), bf16[8,128,400]{1,2,0:T(8,128)(2,1)S(1)}, u32[]{:S(2)}, u32[]{:S(2)}) async-start(bf16[8,128,400]{1,2,0:T(8,128)(2,1)} %copy_bitcast_fusion), calls=%async_computation.1 | async-start | bytes 1638400 | tf_op jit(solution)/shard_map/all_to_all | solution.py:52
  110.0 227.2 %reduce-scatter.8.cloned.1.call-start = ((), (), s32[]{:S(2)}) async-start(), calls=%async_computation.6 | async-start | bytes 14745600 | tf_op jit(solution)/shard_map/reduce_scatter | solution.py:66
  160.4 1.5 copy-start.4
  161.9 23.9 %copy-start.6 = (f32[1024]{0:T(1024)S(1)}, f32[1024]{0:T(1024)}, u32[]{:S(2)}) copy-start(f32[1024]{0:T(1024)} %param.12) | copy-start | bytes 12292
  185.7 5.3 %copy-start.9 = (f32[128]{0:T(128)S(1)}, f32[128]{0:T(128)}, u32[]{:S(2)}) copy-start(f32[128]{0:T(128)} %multiply_reduce_fusion) | copy-start | bytes 1540
  191.0 0.6 copy-start.7
  191.6 0.9 copy-start.1
  199.1 308.8 %reduce-scatter.10.cloned.1.call-start = ((), (), s32[]{:S(2)}) async-start(), calls=%async_computation.7 | async-start | bytes 2162688
  340.0 0.7 copy-start.8
  340.0 1.2 copy-start.2
Sparse Core Ops, SparseCore 0:
  20.2 80.1 reduce-scatter.5
  102.3 83.3 all-gather.1
  199.2 137.8 reduce-scatter.7
  340.2 167.6 reduce-scatter.9
where the time goes:
time: 517 us; the launch traced here: 516 us
  waiting for transfers between devices  449 us (87%)
  matrix products  27.4 us (5%)
  between operations  13.8 us (3%)
  local copies, waits for them, and re-layouts  10.4 us (2%)
  other arithmetic  8.01 us (2%)
  starting transfers between devices  7.26 us (1%)
    unnamed x5, waiting for transfers between devices  162 us
    reduce_scatter x1, waiting for transfers between devices, shards(): lax.psum_scatter(grad_full, 'tensor', scatter_dimension=1, tiled=True)  138 us
    reduce_scatter x1, waiting for transfers between devices, teacher_columns(): lax.psum_scatter(partial_sum.astype(jnp.bfloat16), 'tensor', scatter_dime...  78.8 us
    all_to_all x1, waiting for transfers between devices, shards(): lax.all_to_all(feature_block, 'tensor', split_axis=0, concat_axis=1, tile...  50.1 us
    all_gather x1, waiting for transfers between devices, shards(): full_head = lax.all_gather(head_weight, 'tensor', axis=1, tiled=True)  19.8 us
    dot_general x1, matrix products, teacher_columns(): jnp.dot(teacher_hidden, down_weight, preferred_element_type=jnp.float32)  11.5 us
  transfers between devices with their start and end apart: 5, of which 5 were waited for; matrix products, arithmetic and copies ran while one was open for 3% of the time, Pallas kernels for 0%

commit v1 on v0

--- a/solution.py
+++ b/solution.py
@@ -47,25 +47,33 @@
 def shards(
     teacher_hidden, down_weight, teacher_resid, layer_scale, student_x, norm_gain, head_weight
 ):
-    normed, inverse, normed_out = normalize(student_x, norm_gain)
-    feature_block = teacher_columns(teacher_hidden, down_weight, teacher_resid, layer_scale)
-    target = lax.all_to_all(feature_block, "tensor", split_axis=0, concat_axis=1, tiled=True)
-    full_head = lax.all_gather(head_weight, "tensor", axis=1, tiled=True)
-    predicted = jnp.dot(normed_out, full_head, preferred_element_type=jnp.float32)
+    own_tokens = student_x.shape[0]
+    group_x = lax.all_gather(student_x, "tensor", axis=0, tiled=True)
+    _, _, group_out = normalize(group_x, norm_gain)
+    normed, inverse, _ = normalize(student_x, norm_gain)
+    predicted = jnp.dot(group_out, head_weight, preferred_element_type=jnp.float32)
+    target = teacher_columns(teacher_hidden, down_weight, teacher_resid, layer_scale)
     target_wide = target.astype(jnp.float32)
-    losses, pred_grad = cosine_parts(
-        predicted,
-        target_wide,
-        jnp.sum(predicted * target_wide, axis=1),
-        jnp.sum(predicted * predicted, axis=1),
-        jnp.sum(target_wide * target_wide, axis=1),
+    stats = lax.psum(
+        jnp.stack(
+            [
+                jnp.sum(predicted * target_wide, axis=1),
+                jnp.sum(predicted * predicted, axis=1),
+                jnp.sum(target_wide * target_wide, axis=1),
+            ]
+        ),
+        "tensor",
     )
-    grad_full = lax.dot_general(
-        normed_out, pred_grad, (((0,), (0,)), ((), ())), preferred_element_type=jnp.float32
+    losses, pred_grad = cosine_parts(predicted, target_wide, stats[0], stats[1], stats[2])
+    losses = lax.dynamic_slice_in_dim(losses, lax.axis_index("tensor") * own_tokens, own_tokens)
+    back_part = lax.dot_general(
+        pred_grad, head_weight, (((1,), (1,)), ((), ())), preferred_element_type=jnp.float32
     )
-    grad_block = lax.psum_scatter(grad_full, "tensor", scatter_dimension=1, tiled=True)
-    back_grad = lax.dot_general(
-        pred_grad, full_head, (((1,), (1,)), ((), ())), preferred_element_type=jnp.float32
+    back_grad = lax.psum_scatter(
+        back_part.astype(jnp.bfloat16), "tensor", scatter_dimension=0, tiled=True
+    ).astype(jnp.float32)
+    grad_block = lax.dot_general(
+        group_out, pred_grad, (((0,), (0,)), ((), ())), preferred_element_type=jnp.float32
     )
     head_grad = lax.psum_scatter(grad_block, "dp", scatter_dimension=0, tiled=True).astype(
         jnp.bfloat16

time: 517 us -> 387 us (0.75)
  waiting for transfers between devices: 449 us -> 302 us
  blocking collectives: 0 us -> 29.8 us
  starting transfers between devices: 7.26 us -> 0.16 us
  matrix products: 27.4 us -> 21.9 us
    unnamed x5 -> x4, waiting for transfers between devices: 162 us -> 0.73 us
    reduce_scatter x1 -> x2, waiting for transfers between devices: 138 us -> 199 us  [the longest x1 162 us: shards(): lax.psum_scatter(grad_block, 'dp', scatter_dimension=0, tiled=True)]
    all_to_all x1 -> x0, waiting for transfers between devices: 50.1 us -> none  [shards(): lax.all_to_all(feature_block, 'tensor', split_axis=0, concat_axis=1, tile...]
    psum x0 -> x1, blocking collectives: none -> 29.8 us  [shards(): lax.psum(jnp.stack([jnp.sum(predicted * target_wide, axis=1), jnp.sum(pre...]
    all_to_all x1 -> x0, starting transfers between devices: 7.14 us -> none  [shards(): lax.all_to_all(feature_block, 'tensor', split_axis=0, concat_axis=1, tile...]
    all_gather x1, waiting for transfers between devices: 19.8 us -> 26.8 us  [shards(): group_x = lax.all_gather(student_x, 'tensor', axis=0, tiled=True)]
    dot_general x3, matrix products: 15.9 us -> 10.4 us  [the longest x1 4.71 us: shards(): jnp.dot(group_out, head_weight, preferred_element_type=jnp.float32)]
  transfers between devices with their start and end apart: 5 -> 4, of which waited for: 5 -> 4; matrix products, arithmetic and copies ran while one was open for 3% -> 5% of each run, Pallas kernels for 0% -> 0%
where the time goes in v1:
time: 387 us; the launch traced here: 382 us
  waiting for transfers between devices  302 us (78%)
  blocking collectives  29.8 us (8%)
  matrix products  21.9 us (6%)
  between operations  13.8 us (4%)
  other arithmetic  9.31 us (2%)
  local copies, waits for them, and re-layouts  5.32 us (1%)
    reduce_scatter x1, waiting for transfers between devices, shards(): lax.psum_scatter(grad_block, 'dp', scatter_dimension=0, tiled=True)  162 us
    reduce_scatter x1, waiting for transfers between devices, teacher_columns(): lax.psum_scatter(partial_sum.astype(jnp.bfloat16), 'tensor', scatter_dime...  74.9 us
    reduce_scatter x1, waiting for transfers between devices, shards(): lax.psum_scatter(back_part.astype(jnp.bfloat16), 'tensor', scatter_dimens...  37.3 us
    psum x1, blocking collectives, shards(): lax.psum(jnp.stack([jnp.sum(predicted * target_wide, axis=1), jnp.sum(pre...  29.8 us
    all_gather x1, waiting for transfers between devices, shards(): group_x = lax.all_gather(student_x, 'tensor', axis=0, tiled=True)  26.8 us
    dot_general x1, matrix products, teacher_columns(): jnp.dot(teacher_hidden, down_weight, preferred_element_type=jnp.float32)  11.5 us
  transfers between devices with their start and end apart: 4, of which 4 were waited for; matrix products, arithmetic and copies ran while one was open for 5% of the time, Pallas kernels for 0%

profile of v1, /device:TPU:64, one launch (start us, length us, event | category | flops | bytes accessed | tf_op | source)
XLA Modules:
  0.0 382.1 jit_solution(8533789249694668377)
XLA Ops:
  7.2 0.0 all-gather.2.cloned.1.call-start
  7.2 0.7 all-gather.2.cloned.1.call-update
  7.9 0.0 reduce-scatter.4.cloned.1.call-start
  8.0 0.6 copy-done
  8.6 11.5 %convolution_convert_fusion = bf16[1024,3200]{0,1:T(8,128)(2,1)} fusion(bf16[1024,800]{0,1:T(8,128)(2,1)S(1)} %copy-done, bf16[800,3200]{1,0:T(8,128)(2,1)} %param.8), kind=kOutput, calls=%fused_computation | convolution fusion | flops 5246156800 | bytes 13312000 | tf_op jit(solution)/shard_map/dot_general | solution.py:39
  20.1 0.0 reduce-scatter.4.cloned.1.call-update
  20.1 0.0 reduce-scatter.8.cloned.1.call-start
  20.2 0.8 dynamic_slice.6
  20.9 26.8 %all-gather.2.cloned.1.call-done = bf16[1024,1024]{1,0:T(8,128)(2,1)} async-done(((bf16[128,1024]{1,0:T(8,128)(2,1)}), bf16[1024,1024]{1,0:T(8,128)(2,1)}) %all-gather.2.cloned.1.call-update) | async-done | bytes 2097168 | tf_op jit(solution)/shard_map/all_gather | solution.py:51
  47.7 2.1 convert_reduce_fusion
  49.8 0.1 copy-done.1
  49.9 0.7 fusion.2
  50.6 74.9 %reduce-scatter.4.cloned.1.call-done = bf16[1024,400]{0,1:T(8,128)(2,1)} async-done(((bf16[1024,3200]{0,1:T(8,128)(2,1)}), bf16[1024,400]{0,1:T(8,128)(2,1)}) %reduce-scatter.4.cloned.1.call-update) | async-done | bytes 819216 | tf_op jit(solution)/shard_map/reduce_scatter | solution.py:40
  125.5 4.7 %fusion.5 = (f32[1024]{0:T(1024)S(1)}, f32[1024]{0:T(1024)S(1)}, f32[1024]{0:T(1024)S(1)}, bf16[1024,400]{0,1:T(8,128)(2,1)}, f32[1024,400]{0,1:T(8,128)S(1)}) fusion(bf16[1024,400]{0,1:T(8,128)(2,1)} %reduce-scatter.4.cloned.1.call-done, f32[400]{0:T(512)S(1)} %dynamic_slice.6, bf16[1024,400]{0,1:T(8,128)(2,1)} %param.9, bf16[1024,400]{0,1:T(8,128)(2,1)} %param.13, ...), kind=kOutput, calls=%fused_computation.12 | convolution fusion | flops 849015808 | bytes 7038528 | tf_op jit(solution)/shard_map/dot_general | solution.py:54
  130.3 29.8 %psum.7 = f32[3,1024]{1,0:T(4,128)S(1)} all-reduce(f32[3,1024]{1,0:T(4,128)S(1)} %pad_maximum_fusion), channel_id=1, replica_groups=mesh['dp'=32,'tensor'=8] {'tensor'}, use_global_device_ids=true, to_apply=%region_6.0 | all-reduce | flops 3072 | bytes 24576 | tf_op jit(solution)/shard_map/psum | solution.py:57
  160.1 1.6 fusion.8
  161.7 0.9 copy-done.4
  162.6 3.1 fusion.19
  165.7 0.0 reduce-scatter.8.cloned.1.call-update
  165.7 0.0 reduce-scatter.6.cloned.1.call-start
  165.8 1.1 copy-done.5
  166.8 0.2 copy-done.7
  167.1 2.6 convolution_convert_fusion.1
  169.7 0.9 copy-done.3
  170.6 0.1 convert_reduce_fusion.1
  170.7 0.2 fusion.17
  171.0 0.6 dynamic_slice.7
  171.6 162.1 %reduce-scatter.8.cloned.1.call-done = f32[32,400]{1,0:T(8,128)} async-done(((f32[1024,400]{1,0:T(8,128)}), f32[32,400]{1,0:T(8,128)}) %reduce-scatter.8.cloned.1.call-update) | async-done | bytes 51216 | tf_op jit(solution)/shard_map/reduce_scatter | solution.py:78
  333.7 1.5 convert_element_type.51
  335.2 37.3 %reduce-scatter.6.cloned.1.call-done = bf16[128,1024]{1,0:T(8,128)(2,1)} async-done(((bf16[1024,1024]{1,0:T(8,128)(2,1)}), bf16[128,1024]{1,0:T(8,128)(2,1)}) %reduce-scatter.6.cloned.1.call-update) | async-done | bytes 262160 | tf_op jit(solution)/shard_map/reduce_scatter | solution.py:72
  372.5 1.2 fusion.18
  373.6 1.9 fusion.16
  (20 shorter events, 0.1 us)
Async XLA Ops:
  7.2 1.4 copy-start
  7.2 40.5 %all-gather.2.cloned.1.call-start = ((), (), s32[]{:S(2)}) async-start(), calls=%async_computation.3 | async-start | bytes 2359296 | tf_op jit(solution)/shard_map/all_gather | solution.py:51
  7.9 117.6 %reduce-scatter.4.cloned.1.call-start = ((), (), s32[]{:S(2)}) async-start(), calls=%async_computation.4 | async-start | bytes 7372800 | tf_op jit(solution)/shard_map/reduce_scatter | solution.py:40
  20.1 313.6 %reduce-scatter.8.cloned.1.call-start = ((), (), s32[]{:S(2)}) async-start(), calls=%async_computation.6 | async-start | bytes 2162688 | tf_op jit(solution)/shard_map/reduce_scatter | solution.py:78
  20.9 104.6 %copy-start.6 = (f32[1024]{0:T(1024)S(1)}, f32[1024]{0:T(1024)}, u32[]{:S(2)}) copy-start(f32[1024]{0:T(1024)} %param.12) | copy-start | bytes 12292
  47.7 2.2 copy-start.1
  160.0 2.6 copy-start.2
  161.7 0.9 copy-start.4
  165.7 1.1 copy-start.5
  165.7 1.4 copy-start.7
  165.7 206.7 %reduce-scatter.6.cloned.1.call-start = ((), (), s32[]{:S(2)}) async-start(), calls=%async_computation.5 | async-start | bytes 2359296 | tf_op jit(solution)/shard_map/reduce_scatter | solution.py:72
  169.7 0.9 copy-start.3
Sparse Core Ops, SparseCore 0:
  9.9 37.7 all-gather.1
  50.3 75.2 reduce-scatter.3
  165.8 167.8 reduce-scatter.7
  336.3 36.1 reduce-scatter.5

commit v2 on v0

v2 whole, which is shorter than its diff:
```python
import functools

import jax
import jax.numpy as jnp
from jax import lax
from jax.experimental import pallas as pl
from jax.experimental.pallas import tpu as pltpu
from jax.sharding import PartitionSpec as P

MESH = pl.DeviceIdType.MESH
F32 = jnp.float32
BF16 = jnp.bfloat16
epsilon = 1e-06

DT = 3200
HALF = 1664
STEP = 1536
WIDE = 512
OUTW = 896
CH = 2


def wide(value):
    return value.astype(F32)


def kernel(
    hid_hbm, w_hbm, res_hbm, ls_ref, x_hbm, gain_ref, head_hbm,
    loss_ref, igrad_ref, hgrad_ref,
    hid, w, res, hrow, part, cs, cr, zs, ra, rb, fa, fb, hw, hd, xs, nb, nt, pr, pg,
    st, sr, bp, br, gs, r1, f1, s1, r2, s2, rz, hgs,
    lsem, ssem, rsem,
):
    d = lax.axis_index("dp")
    t = lax.axis_index("tensor")
    zl, x, y = d // 16, (d // 4) % 4, d % 4
    p, c = t // 2, t % 2
    p1, p2, p3 = p + 1 - 2 * (p % 2), (p + 2) % 4, 3 - p
    peer = 1 - c

    def at(zl=zl, x=x, y=y, p=p, c=c):
        return {"dp": zl * 16 + x * 4 + y, "tensor": p * 2 + c}

    counts = [0]

    def ids(n):
        first = counts[0]
        counts[0] += n
        return first

    def remote(src, dst, j, device):
        return pltpu.make_async_remote_copy(
            src_ref=src, dst_ref=dst, send_sem=ssem.at[j], recv_sem=rsem.at[j],
            device_id=device, device_id_type=MESH,
        )

    row_block = x * 4 + y
    loads = [
        pltpu.make_async_copy(
            head_hbm.at[pl.ds(pl.multiple_of(row_block * 64, 64), 64)], hrow, lsem.at[0]
        ),
        pltpu.make_async_copy(x_hbm, xs.at[c], lsem.at[1]),
        pltpu.make_async_copy(w_hbm, w, lsem.at[2]),
        pltpu.make_async_copy(hid_hbm, hid, lsem.at[3]),
        pltpu.make_async_copy(res_hbm, res, lsem.at[4]),
    ]
    for load in loads:
        load.start()

    barrier = pltpu.get_barrier_semaphore()
    zz = p * 2 + zl
    greeted = [at(c=peer)]
    for o in range(1, 8):
        other = (zz + o) % 8
        greeted.append(at(zl=other % 2, p=other // 2))
    for o in range(1, 4):
        greeted.append(at(x=(x + o) % 4))
        greeted.append(at(y=(y + o) % 4))
    for device in greeted:
        pl.semaphore_signal(barrier, inc=1, device_id=device, device_id_type=MESH)

    spot = lax.broadcasted_iota(jnp.int32, (400, WIDE), 1)
    sel = (spot == lax.broadcasted_iota(jnp.int32, (400, WIDE), 0) + 16 * t).astype(BF16)
    hw[0] = jnp.zeros((64, WIDE), BF16)
    hw[9] = jnp.zeros((64, WIDE), BF16)
    loads[0].wait()
    hw[1 + t] = jnp.dot(hrow[...], sel, preferred_element_type=F32).astype(BF16)

    pl.semaphore_wait(barrier, len(greeted))

    x_id = ids(1)

    def x_copy():
        return remote(xs.at[c], xs.at[c], x_id, at(c=peer))

    loads[1].wait()
    x_copy().start()

    hz_id = ids(3)

    def hz_copy(o):
        return remote(hw.at[1 + t], hw.at[1 + t], hz_id + o - 1, at(p=(p + o) % 4))

    for o in (1, 3, 2):
        hz_copy(o).start()

    hc_id = ids(4)

    def hc_copy(o):
        slot = 1 + 2 * ((p + 4 - o) % 4) + c
        return remote(hw.at[slot], hw.at[slot], hc_id + o, at(c=peer))

    h1_id = ids(6)

    def h1_copy(m, o):
        block = hd.at[x, y, :, pl.ds(896 * m, 896 - 128 * m)]
        device = at(x=(x + o) % 4) if m == 0 else at(y=(y + o) % 4)
        return remote(block, block, h1_id + 3 * m + o - 1, device)

    h2_id = ids(6)

    def h2_copy(m, o):
        if m == 0:
            block, device = hd.at[:, y, :, pl.ds(0, 896)], at(y=(y + o) % 4)
        else:
            block, device = hd.at[x, :, :, pl.ds(896, 768)], at(x=(x + o) % 4)
        return remote(block, block, h2_id + 3 * m + o - 1, device)

    def head_first():
        for o in range(4):
            if o:
                hz_copy(o).wait_recv()
            hc_copy(o).start()
        for o in range(4):
            hc_copy(o).wait_recv()
        for j in range(13):
            tile = hw[1 + 4 * c + j // 3, :, (j % 3) * 128 : (j % 3) * 128 + 128]
            if j % 3 == 0:
                tile = tile + hw[4 * c + j // 3, :, 384:512]
            hd[x, y, :, j * 128 : (j + 1) * 128] = tile
        for o in (1, 3, 2):
            for m in range(2):
                h1_copy(m, o).start()

    def head_second():
        for o in range(1, 4):
            for m in range(2):
                h1_copy(m, o).wait_recv()
        for o in (1, 3, 2):
            for m in range(2):
                h2_copy(m, o).start()

    core_id = ids(4)

    def core_copy(k):
        return remote(cs.at[k], cr.at[k], core_id + k, at(c=peer))

    a_id, b_id = ids(3 * CH), ids(3 * CH)
    rows = 128 // CH

    def a_copy(slot, piece):
        own = pl.ds(piece * rows, rows)
        src = fa.at[own] if slot == 2 else zs.at[slot, own]
        return remote(src, ra.at[slot, own], a_id + slot * CH + piece, at(p=p1))

    def b_copy(slot, piece):
        own = pl.ds(piece * rows, rows)
        src = fb.at[own] if slot == 2 else zs.at[2 * slot, pl.ds(128 + piece * rows, rows)]
        return remote(src, rb.at[slot, own], b_id + slot * CH + piece, at(p=p3))

    for load in loads[2:]:
        load.wait()

    def teacher_step(k, carry):
        q = jnp.where(k == 0, p2, jnp.where(k == 1, p1, jnp.where(k == 2, p3, p)))
        tokens = pl.ds(pl.multiple_of(q * 256, 256), 256)
        hidden = hid[tokens, :]
        for low, high in ((0, STEP), (STEP, DT)):
            part[:, low:high] = (
                jnp.dot(hidden, w[:, low:high], preferred_element_type=F32) * ls_ref[:, low:high]
            )
        window = pl.ds(pl.multiple_of(384 * t, 128), WIDE)
        part[:, window] += jnp.dot(res[tokens, :], sel, preferred_element_type=F32)
        cs[k] = part[:, pl.ds(pl.multiple_of(STEP * peer, 128), HALF)].astype(BF16)
        core_copy(k).start()
        core_copy(k).wait_recv()
        own = part[:, pl.ds(pl.multiple_of(STEP * c, 128), HALF)]
        zs[k] = (own + wide(cr[k])).astype(BF16)

        @pl.when(k == 0)
        def _():
            for piece in range(CH):
                a_copy(0, piece).start()
                b_copy(0, piece).start()

        @pl.when(k == 1)
        def _():
            for piece in range(CH):
                a_copy(1, piece).start()
            head_first()

        @pl.when(k == 3)
        def _():
            head_second()

        return carry

    lax.fori_loop(0, 4, teacher_step, 0)

    def normalize(values):
        centered = values - jnp.mean(values, axis=1, keepdims=True)
        inverse = lax.rsqrt(jnp.mean(centered * centered, axis=1, keepdims=True) + epsilon)
        return centered * inverse, inverse

    x_copy().wait_recv()
    for h in range(2):
        normed, _ = normalize(wide(xs[h]))
        out = (normed * gain_ref[...]).astype(BF16)
        nb[h * 128 : (h + 1) * 128, :] = out
        nt[:, h * 128 : (h + 1) * 128] = jnp.transpose(wide(out)).astype(BF16)

    for piece in range(CH):
        low = piece * rows
        a_copy(0, piece).wait_recv()
        fb[low : low + rows, :] = (
            wide(zs[2, low : low + rows, :]) + wide(ra[0, low : low + rows, :])
        ).astype(BF16)
        b_copy(2, piece).start()
        b_copy(1, piece).start()
        b_copy(0, piece).wait_recv()
        fa[low : low + rows, :] = (
            wide(zs[1, 128 + low : 128 + low + rows, :]) + wide(rb[0, low : low + rows, :])
        ).astype(BF16)
        a_copy(2, piece).start()

    for o in range(1, 4):
        for m in range(2):
            h2_copy(m, o).wait_recv()
    head = hd[...].reshape(1024, HALF)
    pr[...] = jnp.dot(nb[...], head, preferred_element_type=F32)

    lane = lax.broadcasted_iota(jnp.int32, (1, HALF), 1)
    mine = (lane >= 128 * c).astype(F32)
    small = lax.broadcasted_iota(jnp.int32, (128, 128), 1)

    stat_id = ids(2)

    def stat_copy(h):
        return remote(st.at[h], sr.at[h], stat_id + h, at(c=peer))

    def finish(h):
        block = slice(h * 128, (h + 1) * 128)
        one, two = (ra, rb) if h == 0 else (rb, ra)
        for piece in range(CH):
            (a_copy if h == 0 else b_copy)(1, piece).wait_recv()
            (b_copy if h == 0 else a_copy)(2, piece).wait_recv()
        total = wide(zs[3, block, :]) + wide(one[1]) + wide(two[2])
        target = wide(total.astype(BF16))
        predicted = pr[block, :]
        masked = predicted * mine
        inner = jnp.sum(masked * target, axis=1, keepdims=True)
        square = jnp.sum(masked * predicted, axis=1, keepdims=True)
        aim = jnp.sum(target * target * mine, axis=1, keepdims=True)
        st[h] = jnp.where(small == 0, inner, jnp.where(small == 1, square, aim))
        stat_copy(h).start()
        stat_copy(h).wait_recv()
        both = st[h] + sr[h]
        inner, square, aim = both[:, 0:1], both[:, 1:2], both[:, 2:3]
        scaling = lax.rsqrt((square + epsilon) * (aim + epsilon))
        cosine = inner * scaling
        pg[block, :] = (
            (cosine / (square + epsilon)) * predicted - scaling * target
        ).astype(BF16)

        @pl.when(c == h)
        def _():
            loss = jnp.broadcast_to(1.0 - cosine, (128, 128))
            loss_ref[...] = jnp.transpose(loss)[0:1, :]

    def back(h):
        bp[h] = lax.dot_general(
            pg[h * 128 : (h + 1) * 128, :] * mine.astype(BF16),
            hd[...].reshape(1024, HALF),
            (((1,), (1,)), ((), ())),
            preferred_element_type=F32,
        )

    finish(0)
    back(0)
    finish(1)

    def grad_step(k, carry):
        piece = jnp.dot(
            nt[pl.ds(pl.multiple_of(k * 128, 128), 128), :], pg[...], preferred_element_type=F32
        ).astype(BF16)
        for j in range(4):
            block = piece[j * 32 : (j + 1) * 32, :]

            @pl.when(k < 4)
            def _():
                gs[0, k, j] = block

            @pl.when(k >= 4)
            def _():
                gs[1, j, k - 4] = block

        return carry

    lax.fori_loop(0, 8, grad_step, 0)

    g_id = ids(12)

    def g_copy(m, way, slot):
        a = x if m == 0 else y
        near, far, last = a + 1 - 2 * (a % 2), (a + 2) % 4, 3 - a
        to = near if way == 0 else last
        device = at(x=to) if m == 0 else at(y=to)
        if slot == 2:
            src = f1.at[m, way]
        else:
            src = gs.at[m, far if slot == 0 else to, pl.ds(2 * way, 2)]
        return remote(src, r1.at[m, way, slot], g_id + m * 6 + way * 3 + slot, device)

    for slot in range(2):
        for m in range(2):
            for way in range(2):
                g_copy(m, way, slot).start()

    back(1)
    back_id = ids(1)

    def back_copy():
        return remote(bp.at[peer], br, back_id, at(c=peer))

    back_copy().start()

    for m in range(2):
        a = x if m == 0 else y
        near, last = a + 1 - 2 * (a % 2), 3 - a
        for way in range(2):
            g_copy(m, way, 0).wait_recv()
        f1[m, 1] = (wide(gs[m, last, 0:2]) + wide(r1[m, 0, 0])).astype(BF16)
        g_copy(m, 1, 2).start()
        f1[m, 0] = (wide(gs[m, near, 2:4]) + wide(r1[m, 1, 0])).astype(BF16)
        g_copy(m, 0, 2).start()

    back_copy().wait_recv()
    normed, inverse = normalize(wide(xs[c]))
    normed_grad = (bp[c] + br[...]) * gain_ref[...]
    igrad_ref[...] = (
        inverse
        * (
            normed_grad
            - jnp.mean(normed_grad, axis=1, keepdims=True)
            - normed * jnp.mean(normed_grad * normed, axis=1, keepdims=True)
        )
    ).astype(BF16)

    g2_id = ids(6)

    def g2_copy(m, o):
        b = y if m == 0 else x
        to = (b + o) % 4
        device = at(y=to) if m == 0 else at(x=to)
        return remote(s1.at[m, to], r2.at[m, o - 1], g2_id + 3 * m + o - 1, device)

    for m in range(2):
        a = x if m == 0 else y
        for way in range(2):
            g_copy(m, way, 1).wait_recv()
        for way in range(2):
            g_copy(m, way, 2).wait_recv()
        for way in range(2):
            s1[m, 2 * way : 2 * way + 2] = (
                wide(gs[m, a, 2 * way : 2 * way + 2])
                + wide(r1[m, way, 1])
                + wide(r1[m, 1 - way, 2])
            ).astype(BF16)
        for o in (1, 3, 2):
            g2_copy(m, o).start()
    for m in range(2):
        b = y if m == 0 else x
        total = wide(s1[m, b])
        for o in range(1, 4):
            g2_copy(m, o).wait_recv()
            total = total + wide(r2[m, o - 1])
        s2[m] = total.astype(BF16)

    g3_id = ids(8)

    def window_of(to):
        return pl.ds(pl.multiple_of(768 * ((to // 2) % 2), 128), OUTW)

    def g3_copy(o):
        to = (zz + o) % 8
        src = s2.at[to % 2, :, window_of(to)]
        return remote(src, rz.at[o], g3_id + o, at(zl=to % 2, p=to // 2))

    for o in (1, 7, 2, 6, 3, 5, 4):

        @pl.when(((zz + o) % 8) // 4 == c)
        def _():
            g3_copy(o).start()

    end_id = ids(1)

    def end_copy():
        return remote(hgs, hgs, end_id, at(c=peer))

    @pl.when(p // 2 == c)
    def _():
        total = wide(s2[zl, :, window_of(zz)])
        for o in range(1, 8):
            g3_copy(o).wait_recv()
            total = total + wide(rz[o])
        hgs[...] = total.astype(BF16)
        end_copy().start()
        end_copy().wait_send()

    @pl.when(p // 2 != c)
    def _():
        end_copy().wait_recv()

    hgrad_ref[...] = hgs[...]

    x_copy().wait_send()
    for o in range(1, 4):
        hz_copy(o).wait_send()
        for m in range(2):
            h1_copy(m, o).wait_send()
            h2_copy(m, o).wait_send()
            g2_copy(m, o).wait_send()
    for o in range(4):
        hc_copy(o).wait_send()
        core_copy(o).wait_send()
    for slot in range(3):
        for piece in range(CH):
            a_copy(slot, piece).wait_send()
            b_copy(slot, piece).wait_send()
        for m in range(2):
            for way in range(2):
                g_copy(m, way, slot).wait_send()
    for h in range(2):
        stat_copy(h).wait_send()
    back_copy().wait_send()
    for o in range(1, 8):

        @pl.when(((zz + o) % 8) // 4 == c)
        def _():
            g3_copy(o).wait_send()


def shards(
    teacher_hidden, down_weight, teacher_resid, layer_scale, student_x, norm_gain, head_weight
):
    hbm = pl.BlockSpec(memory_space=pl.ANY)
    vmem = pl.BlockSpec(memory_space=pltpu.VMEM)
    scratch = [
        ((1024, 800), BF16),
        ((800, DT), BF16),
        ((1024, 400), BF16),
        ((64, 400), BF16),
        ((256, DT), F32),
        ((4, 256, HALF), BF16),
        ((4, 256, HALF), BF16),
        ((4, 256, HALF), BF16),
        ((3, 128, HALF), BF16),
        ((3, 128, HALF), BF16),
        ((128, HALF), BF16),
        ((128, HALF), BF16),
        ((10, 64, WIDE), BF16),
        ((4, 4, 64, HALF), BF16),
        ((2, 128, 1024), BF16),
        ((256, 1024), BF16),
        ((1024, 256), BF16),
        ((256, HALF), F32),
        ((256, HALF), BF16),
        ((2, 128, 128), F32),
        ((2, 128, 128), F32),
        ((2, 128, 1024), F32),
        ((128, 1024), F32),
        ((2, 4, 4, 32, HALF), BF16),
        ((2, 2, 3, 2, 32, HALF), BF16),
        ((2, 2, 2, 32, HALF), BF16),
        ((2, 4, 32, HALF), BF16),
        ((2, 3, 32, HALF), BF16),
        ((2, 32, HALF), BF16),
        ((8, 32, OUTW), BF16),
        ((32, OUTW), BF16),
    ]
    copies = 1 + 3 + 4 + 6 + 6 + 4 + 6 * CH + 2 + 12 + 1 + 6 + 8 + 1
    loss, input_grad, head_grad = pl.pallas_call(
        kernel,
        name="distill",
        out_shape=(
            jax.ShapeDtypeStruct((1, 128), F32),
            jax.ShapeDtypeStruct((128, 1024), BF16),
            jax.ShapeDtypeStruct((32, OUTW), BF16),
        ),
        in_specs=[hbm, hbm, hbm, vmem, hbm, vmem, hbm],
        out_specs=(vmem, vmem, vmem),
        scratch_shapes=[pltpu.VMEM(shape, kind) for shape, kind in scratch]
        + [
            pltpu.SemaphoreType.DMA((5,)),
            pltpu.SemaphoreType.DMA((copies,)),
            pltpu.SemaphoreType.DMA((copies,)),
        ],
        compiler_params=pltpu.CompilerParams(
            collective_id=0, has_side_effects=True, vmem_limit_bytes=60 * 2**20
        ),
        cost_estimate=pl.CostEstimate(
            flops=8_000_000_000, bytes_accessed=10_000_000, transcendentals=1000
        ),
    )(
        teacher_hidden,
        down_weight,
        teacher_resid,
        layer_scale.reshape(1, DT),
        student_x,
        norm_gain.reshape(1, -1),
        head_weight,
    )
    t = lax.axis_index("tensor")
    first = 32 * (t // 2) + 400 * (t % 2)
    head_grad = lax.dynamic_slice_in_dim(head_grad, first, 400, axis=1)
    return (loss.reshape(-1), input_grad, head_grad)


def solution(mesh):
    placed = (
        P("dp", "tensor"),
        P("tensor", None),
        P("dp", "tensor"),
        P(),
        P(("dp", "tensor"), None),
        P(),
        P(None, "tensor"),
    )
    return jax.shard_map(
        shards,
        mesh=mesh,
        in_specs=placed,
        out_specs=(P(("dp", "tensor")), P(("dp", "tensor"), None), P("dp", "tensor")),
        check_vma=False,
    )
```

time: 517 us -> 128 us (0.25)
  the two profiles are of different devices: /device:TPU:64 before, /device:TPU:1 now
where the time goes in v2:
time: 128 us
  Pallas kernels  116 us (91%)
  local copies, waits for them, and re-layouts  11.3 us (9%)
    pallas_call x1, Pallas kernels, shards(): pl.pallas_call(kernel, name='distill', out_shape=(jax.ShapeDtypeStruct((1...  116 us
    unnamed x11, local copies, waits for them, and re-layouts  9.26 us

profile of v2, /device:TPU:1, one launch (start us, length us, event | category | flops | bytes accessed | tf_op | source)
XLA Modules:
  0.0 128.1 jit_solution(17438326158203957114)
XLA Ops:
  0.6 0.0 copy-start
  0.6 0.0 copy-start.2
  0.7 0.0 copy-start.1
  0.7 3.8 %copy.10.hid_hbm = bf16[1024,800]{1,0:T(8,128)(2,1)} copy(bf16[1024,800]{0,1:T(8,128)(2,1)} %param.7) | data formatting | bytes 3276800 | tf_op args[0]
  4.5 0.0 copy-done
  4.5 1.3 %copy.11.res_hbm = bf16[1024,400]{1,0:T(8,128)(2,1)} copy(bf16[1024,400]{0,1:T(8,128)(2,1)S(1)} %copy-done) | data formatting | bytes 1638400 | tf_op args[2]
  5.8 0.0 copy-done.2
  5.8 0.6 reshape.15.ls_ref
  6.4 0.0 copy-done.1
  6.4 1.3 %copy.12.head_hbm = bf16[1024,400]{1,0:T(8,128)(2,1)} copy(bf16[1024,400]{0,1:T(8,128)(2,1)S(1)} %copy-done.1) | data formatting | bytes 1638400 | tf_op args[6]
  7.7 116.1 %distill.1 = (f32[1,128]{1,0:T(1,128)}, bf16[128,1024]{1,0:T(8,128)(2,1)}, bf16[32,896]{1,0:T(8,128)(2,1)}) custom-call(bf16[1024,800]{1,0:T(8,128)(2,1)} %copy.10.hid_hbm, bf16[800,3200]{1,0:T(8,128)(2,1)} %w_hbm.1, bf16[1024,400]{1,0:T(8,128)(2,1)} %copy.11.res_hbm, f32[1,3200]{1,0:T(1,128)} %reshape.15.ls_ref, bf16[128,1024]{1,0:T(8,128)(2,1)} %x_hbm.1, ...), custom_call_target="tpu_custom_call" | custom-call | flops 8000000000 | bytes 10000000 | tf_op jit(solution)/shard_map/distill/pallas_call | solution.py:492
  123.9 1.5 %constant_dynamic-slice_fusion = bf16[32,400]{1,0:T(8,128)(2,1)} fusion(bf16[32,896]{1,0:T(8,128)(2,1)} %get-tuple-element.8, s32[]{:T(128)S(6)} %select_n.16), kind=kLoop, calls=%fused_computation | loop fusion | bytes 51204 | tf_op jit(solution)/shard_map/dynamic_slice | solution.py:525
  125.3 1.1 copy.15
  126.5 1.7 %copy.16 = bf16[128,1024]{1,0:T(8,128)(2,1)} copy(bf16[128,1024]{1,0:T(8,128)(2,1)} %get-tuple-element.13) | data formatting | bytes 524288
Async XLA Ops:
  0.6 3.9 %copy-start = (bf16[1024,400]{0,1:T(8,128)(2,1)S(1)}, bf16[1024,400]{0,1:T(8,128)(2,1)}, u32[]{:S(2)}) copy-start(bf16[1024,400]{0,1:T(8,128)(2,1)} %param.9) | copy-start | bytes 2457604
  0.6 5.2 %copy-start.2 = (f32[3200]{0:T(1024)S(1)}, f32[3200]{0:T(1024)}, u32[]{:S(2)}) copy-start(f32[3200]{0:T(1024)} %param.10) | copy-start | bytes 38404
  0.7 5.8 %copy-start.1 = (bf16[1024,400]{0,1:T(8,128)(2,1)S(1)}, bf16[1024,400]{0,1:T(8,128)(2,1)}, u32[]{:S(2)}) copy-start(bf16[1024,400]{0,1:T(8,128)(2,1)} %param.13) | copy-start | bytes 2457604

commit v3 on v2

--- a/solution.py
+++ b/solution.py
@@ -17,18 +17,22 @@
 STEP = 1536
 WIDE = 512
 OUTW = 896
-CH = 2
+CH = 4
 
 
 def wide(value):
     return value.astype(F32)
+
+
+def across(left, right):
+    return lax.dot_general(left, right, (((0,), (0,)), ((), ())), preferred_element_type=F32)
 
 
 def kernel(
     hid_hbm, w_hbm, res_hbm, ls_ref, x_hbm, gain_ref, head_hbm,
     loss_ref, igrad_ref, hgrad_ref,
-    hid, w, res, hrow, part, cs, cr, zs, ra, rb, fa, fb, hw, hd, xs, nb, nt, pr, pg,
-    st, sr, bp, br, gs, r1, f1, s1, r2, s2, rz, hgs,
+    hid, w, res, hrow, htwo, lsrow, part, cs, cr, zs, ra, rb, fa, fb, hw, hd, xs, nb, nt, pr, pg,
+    squares, tg, losses, st, sr, bp, br, gs, r1, f1, s1, r2, s2, rz, hgs,
     lsem, ssem, rsem,
 ):
     d = lax.axis_index("dp")
@@ -57,7 +61,7 @@
     row_block = x * 4 + y
     loads = [
         pltpu.make_async_copy(
-            head_hbm.at[pl.ds(pl.multiple_of(row_block * 64, 64), 64)], hrow, lsem.at[0]
+            head_hbm.at[:, pl.ds(pl.multiple_of(row_block // 2 * 128, 128), 128)], hrow, lsem.at[0]
         ),
         pltpu.make_async_copy(x_hbm, xs.at[c], lsem.at[1]),
         pltpu.make_async_copy(w_hbm, w, lsem.at[2]),
@@ -84,7 +88,10 @@
     hw[0] = jnp.zeros((64, WIDE), BF16)
     hw[9] = jnp.zeros((64, WIDE), BF16)
     loads[0].wait()
-    hw[1 + t] = jnp.dot(hrow[...], sel, preferred_element_type=F32).astype(BF16)
+    htwo[...] = across(hrow[...], sel)
+    hw[1 + t] = htwo[pl.ds(pl.multiple_of(row_block % 2 * 64, 64), 64), :].astype(BF16)
+    for j in range(25):
+        lsrow[:, j * 128 : (j + 1) * 128] = ls_ref[j : j + 1, :]
 
     pl.semaphore_wait(barrier, len(greeted))
 
@@ -174,13 +181,13 @@
     def teacher_step(k, carry):
         q = jnp.where(k == 0, p2, jnp.where(k == 1, p1, jnp.where(k == 2, p3, p)))
         tokens = pl.ds(pl.multiple_of(q * 256, 256), 256)
-        hidden = hid[tokens, :]
+        hidden = jnp.transpose(hid[:, tokens])
         for low, high in ((0, STEP), (STEP, DT)):
             part[:, low:high] = (
-                jnp.dot(hidden, w[:, low:high], preferred_element_type=F32) * ls_ref[:, low:high]
+                jnp.dot(hidden, w[:, low:high], preferred_element_type=F32) * lsrow[:, low:high]
             )
         window = pl.ds(pl.multiple_of(384 * t, 128), WIDE)
-        part[:, window] += jnp.dot(res[tokens, :], sel, preferred_element_type=F32)
+        part[:, window] += across(res[:, tokens], sel)
         cs[k] = part[:, pl.ds(pl.multiple_of(STEP * peer, 128), HALF)].astype(BF16)
         core_copy(k).start()
         core_copy(k).wait_recv()
@@ -217,7 +224,8 @@
         normed, _ = normalize(wide(xs[h]))
         out = (normed * gain_ref[...]).astype(BF16)
         nb[h * 128 : (h + 1) * 128, :] = out
-        nt[:, h * 128 : (h + 1) * 128] = jnp.transpose(wide(out)).astype(BF16)
+        turned = jnp.transpose(wide(out)).astype(BF16)
+        nt[:, :, :, :, h * 128 : (h + 1) * 128] = turned.reshape(2, 4, 4, 32, 128)
 
     for piece in range(CH):
         low = piece * rows
@@ -241,41 +249,51 @@
 
     lane = lax.broadcasted_iota(jnp.int32, (1, HALF), 1)
     mine = (lane >= 128 * c).astype(F32)
-    small = lax.broadcasted_iota(jnp.int32, (128, 128), 1)
-
-    stat_id = ids(2)
-
-    def stat_copy(h):
-        return remote(st.at[h], sr.at[h], stat_id + h, at(c=peer))
+    small = lax.broadcasted_iota(jnp.int32, (rows, 128), 1)
+
+    stat_id = ids(2 * CH)
+
+    def stat_copy(h, piece):
+        own = pl.ds(piece * rows, rows)
+        return remote(st.at[h, own], sr.at[h, own], stat_id + h * CH + piece, at(c=peer))
+
+    square_all = jnp.sum(pr[...] * pr[...] * mine, axis=1, keepdims=True)
+    squares[...] = jnp.broadcast_to(square_all, (256, 128))
 
     def finish(h):
-        block = slice(h * 128, (h + 1) * 128)
         one, two = (ra, rb) if h == 0 else (rb, ra)
         for piece in range(CH):
             (a_copy if h == 0 else b_copy)(1, piece).wait_recv()
             (b_copy if h == 0 else a_copy)(2, piece).wait_recv()
-        total = wide(zs[3, block, :]) + wide(one[1]) + wide(two[2])
-        target = wide(total.astype(BF16))
-        predicted = pr[block, :]
-        masked = predicted * mine
-        inner = jnp.sum(masked * target, axis=1, keepdims=True)
-        square = jnp.sum(masked * predicted, axis=1, keepdims=True)
-        aim = jnp.sum(target * target * mine, axis=1, keepdims=True)
-        st[h] = jnp.where(small == 0, inner, jnp.where(small == 1, square, aim))
-        stat_copy(h).start()
-        stat_copy(h).wait_recv()
-        both = st[h] + sr[h]
-        inner, square, aim = both[:, 0:1], both[:, 1:2], both[:, 2:3]
-        scaling = lax.rsqrt((square + epsilon) * (aim + epsilon))
-        cosine = inner * scaling
-        pg[block, :] = (
-            (cosine / (square + epsilon)) * predicted - scaling * target
-        ).astype(BF16)
+            own = slice(piece * rows, (piece + 1) * rows)
+            block = slice(h * 128 + piece * rows, h * 128 + (piece + 1) * rows)
+            total = wide(zs[3, block, :]) + wide(one[1, own, :]) + wide(two[2, own, :])
+            target = total.astype(BF16)
+            tg[block, :] = target
+            target = wide(target)
+            masked = target * mine
+            inner = jnp.sum(masked * pr[block, :], axis=1, keepdims=True)
+            aim = jnp.sum(masked * target, axis=1, keepdims=True)
+            st[h, own, :] = jnp.where(
+                small == 0, inner, jnp.where(small == 1, squares[block, :], aim)
+            )
+            stat_copy(h, piece).start()
+        for piece in range(CH):
+            own = slice(piece * rows, (piece + 1) * rows)
+            block = slice(h * 128 + piece * rows, h * 128 + (piece + 1) * rows)
+            stat_copy(h, piece).wait_recv()
+            both = st[h, own, :] + sr[h, own, :]
+            inner, square, aim = both[:, 0:1], both[:, 1:2], both[:, 2:3]
+            scaling = lax.rsqrt((square + epsilon) * (aim + epsilon))
+            cosine = inner * scaling
+            pg[block, :] = (
+                (cosine / (square + epsilon)) * pr[block, :] - scaling * wide(tg[block, :])
+            ).astype(BF16)
+            losses[own, :] = jnp.broadcast_to(1.0 - cosine, (rows, 128))
 
         @pl.when(c == h)
         def _():
-            loss = jnp.broadcast_to(1.0 - cosine, (128, 128))
-            loss_ref[...] = jnp.transpose(loss)[0:1, :]
+            loss_ref[...] = jnp.transpose(losses[...])[0:1, :]
 
     def back(h):
         bp[h] = lax.dot_general(
@@ -289,42 +307,114 @@
     back(0)
     finish(1)
 
-    def grad_step(k, carry):
-        piece = jnp.dot(
-            nt[pl.ds(pl.multiple_of(k * 128, 128), 128), :], pg[...], preferred_element_type=F32
-        ).astype(BF16)
-        for j in range(4):
-            block = piece[j * 32 : (j + 1) * 32, :]
-
-            @pl.when(k < 4)
-            def _():
-                gs[0, k, j] = block
-
-            @pl.when(k >= 4)
-            def _():
-                gs[1, j, k - 4] = block
-
-        return carry
-
-    lax.fori_loop(0, 8, grad_step, 0)
-
-    g_id = ids(12)
-
-    def g_copy(m, way, slot):
+    parts = (pl.ds(0, OUTW), pl.ds(OUTW, HALF - OUTW))
+    g_id = ids(24)
+    axes = []
+    for m in range(2):
         a = x if m == 0 else y
-        near, far, last = a + 1 - 2 * (a % 2), (a + 2) % 4, 3 - a
+        axes.append((a, a + 1 - 2 * (a % 2), (a + 2) % 4, 3 - a))
+
+    def g_copy(n, m, way, slot):
+        a, near, far, last = axes[m]
         to = near if way == 0 else last
         device = at(x=to) if m == 0 else at(y=to)
         if slot == 2:
-            src = f1.at[m, way]
+            src = f1.at[m, way, :, :, parts[n]]
         else:
-            src = gs.at[m, far if slot == 0 else to, pl.ds(2 * way, 2)]
-        return remote(src, r1.at[m, way, slot], g_id + m * 6 + way * 3 + slot, device)
-
-    for slot in range(2):
+            src = gs.at[m, far if slot == 0 else to, pl.ds(2 * way, 2), :, parts[n]]
+        dst = r1.at[m, way, slot, :, :, parts[n]]
+        return remote(src, dst, g_id + n * 12 + m * 6 + way * 3 + slot, device)
+
+    def gradient(n, turn):
+        ax, ay = axes[0][turn], axes[1][turn]
+        left = jnp.concatenate(
+            [nt[0, ax].reshape(128, 256), nt[1, :, ay].reshape(128, 256)], axis=0
+        )
+        both = jnp.dot(left, pg[:, parts[n]], preferred_element_type=F32).astype(BF16)
+        gs[0, ax, :, :, parts[n]] = both[0:128].reshape(4, 32, -1)
+        gs[1, ay, :, :, parts[n]] = both[128:256].reshape(4, 32, -1)
+
+    def first_sends(n, slot):
         for m in range(2):
             for way in range(2):
-                g_copy(m, way, slot).start()
+                g_copy(n, m, way, slot).start()
+
+    def forward(n):
+        for m in range(2):
+            a, near, far, last = axes[m]
+            for way in range(2):
+                g_copy(n, m, 1 - way, 0).wait_recv()
+                target, inner = (near, slice(2, 4)) if way == 0 else (last, slice(0, 2))
+                f1[m, way, :, :, parts[n]] = (
+                    wide(gs[m, target, inner, :, parts[n]])
+                    + wide(r1[m, 1 - way, 0, :, :, parts[n]])
+                ).astype(BF16)
+                g_copy(n, m, way, 2).start()
+
+    g2_id = ids(12)
+
+    def g2_copy(n, m, o):
+        b = y if m == 0 else x
+        to = (b + o) % 4
+        device = at(y=to) if m == 0 else at(x=to)
+        return remote(
+            s1.at[m, to, :, parts[n]], r2.at[m, o - 1, :, parts[n]],
+            g2_id + 6 * n + 3 * m + o - 1, device,
+        )
+
+    def second_sends(n):
+        for m in range(2):
+            a = axes[m][0]
+            for slot in (1, 2):
+                for way in range(2):
+                    g_copy(n, m, way, slot).wait_recv()
+            for way in range(2):
+                inner = slice(2 * way, 2 * way + 2)
+                s1[m, inner, :, parts[n]] = (
+                    wide(gs[m, a, inner, :, parts[n]])
+                    + wide(r1[m, way, 1, :, :, parts[n]])
+                    + wide(r1[m, 1 - way, 2, :, :, parts[n]])
+                ).astype(BF16)
+            for o in (1, 3, 2):
+                g2_copy(n, m, o).start()
+
+    def second_sums(n):
+        for m in range(2):
+            total = wide(s1[m, axes[1 - m][0], :, parts[n]])
+            for o in range(1, 4):
+                g2_copy(n, m, o).wait_recv()
+                total = total + wide(r2[m, o - 1, :, parts[n]])
+            s2[m, :, parts[n]] = total.astype(BF16)
+
+    g3_id = ids(8)
+
+    def window_of(to):
+        return pl.ds(pl.multiple_of(768 * ((to // 2) % 2), 128), OUTW)
+
+    def g3_copy(o):
+        to = (zz + o) % 8
+        src = s2.at[to % 2, :, window_of(to)]
+        return remote(src, rz.at[o], g3_id + o, at(zl=to % 2, p=to // 2))
+
+    def third_sends(n):
+        for o in (1, 7, 2, 6, 3, 5, 4):
+            chip = ((zz + o) % 8) // 2
+
+            @pl.when((chip // 2 == c) & (chip % 2 == n))
+            def _():
+                g3_copy(o).start()
+
+    gradient(0, 2)
+    first_sends(0, 0)
+    gradient(0, 1)
+    gradient(0, 3)
+    first_sends(0, 1)
+    gradient(0, 0)
+    for turn in range(4):
+        gradient(1, turn)
+    forward(0)
+    first_sends(1, 0)
+    first_sends(1, 1)
 
     back(1)
     back_id = ids(1)
@@ -333,16 +423,8 @@
         return remote(bp.at[peer], br, back_id, at(c=peer))
 
     back_copy().start()
-
-    for m in range(2):
-        a = x if m == 0 else y
-        near, last = a + 1 - 2 * (a % 2), 3 - a
-        for way in range(2):
-            g_copy(m, way, 0).wait_recv()
-        f1[m, 1] = (wide(gs[m, last, 0:2]) + wide(r1[m, 0, 0])).astype(BF16)
-        g_copy(m, 1, 2).start()
-        f1[m, 0] = (wide(gs[m, near, 2:4]) + wide(r1[m, 1, 0])).astype(BF16)
-        g_copy(m, 0, 2).start()
+    second_sends(0)
+    forward(1)
 
     back_copy().wait_recv()
     normed, inverse = normalize(wide(xs[c]))
@@ -356,51 +438,11 @@
         )
     ).astype(BF16)
 
-    g2_id = ids(6)
-
-    def g2_copy(m, o):
-        b = y if m == 0 else x
-        to = (b + o) % 4
-        device = at(y=to) if m == 0 else at(x=to)
-        return remote(s1.at[m, to], r2.at[m, o - 1], g2_id + 3 * m + o - 1, device)
-
-    for m in range(2):
-        a = x if m == 0 else y
-        for way in range(2):
-            g_copy(m, way, 1).wait_recv()
-        for way in range(2):
-            g_copy(m, way, 2).wait_recv()
-        for way in range(2):
-            s1[m, 2 * way : 2 * way + 2] = (
-                wide(gs[m, a, 2 * way : 2 * way + 2])
-                + wide(r1[m, way, 1])
-                + wide(r1[m, 1 - way, 2])
-            ).astype(BF16)
-        for o in (1, 3, 2):
-            g2_copy(m, o).start()
-    for m in range(2):
-        b = y if m == 0 else x
-        total = wide(s1[m, b])
-        for o in range(1, 4):
-            g2_copy(m, o).wait_recv()
-            total = total + wide(r2[m, o - 1])
-        s2[m] = total.astype(BF16)
-
-    g3_id = ids(8)
-
-    def window_of(to):
-        return pl.ds(pl.multiple_of(768 * ((to // 2) % 2), 128), OUTW)
-
-    def g3_copy(o):
-        to = (zz + o) % 8
-        src = s2.at[to % 2, :, window_of(to)]
-        return remote(src, rz.at[o], g3_id + o, at(zl=to % 2, p=to // 2))
-
-    for o in (1, 7, 2, 6, 3, 5, 4):
-
-        @pl.when(((zz + o) % 8) // 4 == c)
-        def _():
-            g3_copy(o).start()
+    second_sums(0)
+    third_sends(0)
+    second_sends(1)
+    second_sums(1)
+    third_sends(1)
 
     end_id = ids(1)
 
@@ -429,7 +471,8 @@
         for m in range(2):
             h1_copy(m, o).wait_send()
             h2_copy(m, o).wait_send()
-            g2_copy(m, o).wait_send()
+            for n in range(2):
+                g2_copy(n, m, o).wait_send()
     for o in range(4):
         hc_copy(o).wait_send()
         core_copy(o).wait_send()
@@ -439,15 +482,27 @@
             b_copy(slot, piece).wait_send()
         for m in range(2):
             for way in range(2):
-                g_copy(m, way, slot).wait_send()
+                for n in range(2):
+                    g_copy(n, m, way, slot).wait_send()
     for h in range(2):
-        stat_copy(h).wait_send()
+        for piece in range(CH):
+            stat_copy(h, piece).wait_send()
     back_copy().wait_send()
     for o in range(1, 8):
 
         @pl.when(((zz + o) % 8) // 4 == c)
         def _():
             g3_copy(o).wait_send()
+
+
+def place(loss_ref, igrad_ref, hgrad_ref, loss_out, igrad_out, hgrad_out):
+    loss_out[...] = loss_ref[...]
+    igrad_out[...] = igrad_ref[...]
+    t = lax.axis_index("tensor")
+    first = 32 * (t // 2) + 400 * (t % 2)
+    row = lax.broadcasted_iota(jnp.int32, (OUTW, 400), 0)
+    pick = (row == lax.broadcasted_iota(jnp.int32, (OUTW, 400), 1) + first).astype(BF16)
+    hgrad_out[...] = jnp.dot(hgrad_ref[...], pick, preferred_element_type=F32).astype(BF16)
 
 
 def shards(
@@ -456,10 +511,12 @@
     hbm = pl.BlockSpec(memory_space=pl.ANY)
     vmem = pl.BlockSpec(memory_space=pltpu.VMEM)
     scratch = [
-        ((1024, 800), BF16),
+        ((800, 1024), BF16),
         ((800, DT), BF16),
-        ((1024, 400), BF16),
-        ((64, 400), BF16),
+        ((400, 1024), BF16),
+        ((400, 128), BF16),
+        ((128, WIDE), F32),
+        ((1, DT), F32),
         ((256, DT), F32),
         ((4, 256, HALF), BF16),
         ((4, 256, HALF), BF16),
@@ -472,9 +529,12 @@
         ((4, 4, 64, HALF), BF16),
         ((2, 128, 1024), BF16),
         ((256, 1024), BF16),
-        ((1024, 256), BF16),
+        ((2, 4, 4, 32, 256), BF16),
         ((256, HALF), F32),
         ((256, HALF), BF16),
+        ((256, 128), F32),
+        ((256, HALF), BF16),
+        ((128, 128), F32),
         ((2, 128, 128), F32),
         ((2, 128, 128), F32),
         ((2, 128, 1024), F32),
@@ -488,7 +548,7 @@
         ((8, 32, OUTW), BF16),
         ((32, OUTW), BF16),
     ]
-    copies = 1 + 3 + 4 + 6 + 6 + 4 + 6 * CH + 2 + 12 + 1 + 6 + 8 + 1
+    copies = 1 + 3 + 4 + 6 + 6 + 4 + 6 * CH + 2 * CH + 24 + 12 + 8 + 1 + 1
     loss, input_grad, head_grad = pl.pallas_call(
         kernel,
         name="distill",
@@ -512,17 +572,25 @@
             flops=8_000_000_000, bytes_accessed=10_000_000, transcendentals=1000
         ),
     )(
-        teacher_hidden,
+        teacher_hidden.T,
         down_weight,
-        teacher_resid,
-        layer_scale.reshape(1, DT),
+        teacher_resid.T,
+        layer_scale.reshape(25, 128),
         student_x,
         norm_gain.reshape(1, -1),
-        head_weight,
+        head_weight.T,
     )
-    t = lax.axis_index("tensor")
-    first = 32 * (t // 2) + 400 * (t % 2)
-    head_grad = lax.dynamic_slice_in_dim(head_grad, first, 400, axis=1)
+    loss, input_grad, head_grad = pl.pallas_call(
+        place,
+        name="place",
+        out_shape=(
+            jax.ShapeDtypeStruct((1, 128), F32),
+            jax.ShapeDtypeStruct((128, 1024), BF16),
+            jax.ShapeDtypeStruct((32, 400), BF16),
+        ),
+        in_specs=[vmem, vmem, vmem],
+        out_specs=(vmem, vmem, vmem),
+    )(loss, input_grad, head_grad)
     return (loss.reshape(-1), input_grad, head_grad)
 
 

time: 128 us -> 111 us (0.87)
  the two profiles are of different devices: /device:TPU:1 before, /device:TPU:64 now
where the time goes in v3:
time: 111 us
  Pallas kernels  110 us (99%)
    pallas_call x1, Pallas kernels, shards(): pl.pallas_call(kernel, name='distill', out_shape=(jax.ShapeDtypeStruct((1...  108 us

profile of v3, /device:TPU:64, one launch (start us, length us, event | category | flops | bytes accessed | tf_op | source)
XLA Modules:
  0.0 110.7 jit_solution(11609836897761074968)
XLA Ops:
  0.6 108.2 %distill.1 = (f32[1,128]{1,0:T(1,128)}, bf16[128,1024]{1,0:T(8,128)(2,1)}, bf16[32,896]{1,0:T(8,128)(2,1)}) custom-call(bf16[800,1024]{1,0:T(8,128)(2,1)} %bitcast.6, bf16[800,3200]{1,0:T(8,128)(2,1)} %w_hbm.1, bf16[400,1024]{1,0:T(8,128)(2,1)} %bitcast.7, f32[25,128]{1,0:T(8,128)} %bitcast.9, bf16[128,1024]{1,0:T(8,128)(2,1)} %x_hbm.1, f32[1,1024]{1,0:T(1,128)} %bitcast.10, ...), custom_call_target="tpu_custom_call" | custom-call | flops 8000000000 | bytes 10000000 | tf_op jit(solution)/shard_map/distill/pallas_call | solution.py:552
  108.8 1.9 %place.1 = (f32[1,128]{1,0:T(1,128)}, bf16[128,1024]{1,0:T(8,128)(2,1)}, bf16[32,400]{1,0:T(8,128)(2,1)}) custom-call(f32[1,128]{1,0:T(1,128)} %get-tuple-element.9.loss_ref, bf16[128,1024]{1,0:T(8,128)(2,1)} %get-tuple-element.10.igrad_ref, bf16[32,896]{1,0:T(8,128)(2,1)} %get-tuple-element.11.hgrad_ref), custom_call_target="tpu_custom_call" | custom-call | tf_op jit(solution)/shard_map/place/pallas_call | solution.py:583

commit v4 on v3

v4 whole, which is shorter than its diff:
```python
import functools

import jax
import jax.numpy as jnp
from jax import lax
from jax.experimental import pallas as pl
from jax.experimental.pallas import tpu as pltpu
from jax.sharding import PartitionSpec as P

MESH = pl.DeviceIdType.MESH
F32 = jnp.float32
BF16 = jnp.bfloat16
epsilon = 1e-06

DT = 3200
HALF = 1664
STEP = 1536
WIDE = 512
CH = 2


def wide(value):
    return value.astype(F32)


def across(left, right):
    return lax.dot_general(left, right, (((0,), (0,)), ((), ())), preferred_element_type=F32)


def kernel(
    hid_hbm, w_hbm, res_hbm, ls_ref, x_hbm, gain_ref, head_hbm,
    loss_ref, igrad_ref, hgrad_ref,
    hid, hq, rq, w, res, hrow, htwo, lsrow, part, cs, cr, zs, ra, rb, fa, fb, hw, hd, xs, nb, nt, pr, pg,
    squares, tg, losses, st, sr, bp, br, gs0, gs1, r10, r11, f10, f11, s10, s11, r20, r21, s2, rz,
    lsem, ssem, rsem,
):
    d = lax.axis_index("dp")
    t = lax.axis_index("tensor")
    zl, x, y = d // 16, (d // 4) % 4, d % 4
    p, c = t // 2, t % 2
    p1, p2, p3 = p + 1 - 2 * (p % 2), (p + 2) % 4, 3 - p
    peer = 1 - c

    def at(zl=zl, x=x, y=y, p=p, c=c):
        return {"dp": zl * 16 + x * 4 + y, "tensor": p * 2 + c}

    counts = [0]

    def ids(n):
        first = counts[0]
        counts[0] += n
        return first

    def remote(src, dst, j, device):
        return pltpu.make_async_remote_copy(
            src_ref=src, dst_ref=dst, send_sem=ssem.at[j], recv_sem=rsem.at[j],
            device_id=device, device_id_type=MESH,
        )

    row_block = x * 4 + y
    cuts = ((0, 208), (208, 208), (416, 192), (608, 192))
    loads = [
        pltpu.make_async_copy(hid_hbm, hid, lsem.at[0]),
        pltpu.make_async_copy(res_hbm, res, lsem.at[1]),
        pltpu.make_async_copy(
            head_hbm.at[:, pl.ds(pl.multiple_of(row_block // 2 * 128, 128), 128)], hrow, lsem.at[2]
        ),
        pltpu.make_async_copy(x_hbm, xs.at[c], lsem.at[3]),
    ] + [
        pltpu.make_async_copy(w_hbm.at[pl.ds(low, n)], w.at[pl.ds(low, n)], lsem.at[4 + i])
        for i, (low, n) in enumerate(cuts)
    ]
    for load in (loads[2], loads[3], loads[0], *loads[4:], loads[1]):
        load.start()

    barrier = pltpu.get_barrier_semaphore()
    zz = p * 2 + zl
    greeted = [at(c=peer)]
    for o in range(1, 8):
        other = (zz + o) % 8
        greeted.append(at(zl=other % 2, p=other // 2))
        greeted.append(at(zl=other % 2, p=other // 2, c=peer))
    for o in range(1, 4):
        greeted.append(at(x=(x + o) % 4))
        greeted.append(at(y=(y + o) % 4))
    for device in greeted:
        pl.semaphore_signal(barrier, inc=1, device_id=device, device_id_type=MESH)

    spot = lax.broadcasted_iota(jnp.int32, (400, WIDE), 1)
    sel = (spot == lax.broadcasted_iota(jnp.int32, (400, WIDE), 0) + 16 * t).astype(BF16)
    hw[0] = jnp.zeros((64, WIDE), BF16)
    hw[9] = jnp.zeros((64, WIDE), BF16)
    for j in range(25):
        lsrow[:, j * 128 : (j + 1) * 128] = ls_ref[j : j + 1, :]

    def block_of(k):
        return jnp.where(k == 0, p2, jnp.where(k == 1, p1, jnp.where(k == 2, p3, p)))

    def teacher_half(k, h):
        columns = pl.ds(pl.multiple_of(STEP * h, 128), HALF)
        part[...] = (
            jnp.dot(hq[k], w[:, columns], preferred_element_type=F32) * lsrow[:, columns]
        )

        @pl.when(t // 4 == h)
        def _():
            window = pl.ds(pl.multiple_of(384 * (t % 4), 128), WIDE)
            part[:, window] += wide(rq[k])

        @pl.when((t == 3) & (h == 1))
        def _():
            part[:, 0:128] += wide(rq[k, :, 384:512])

        @pl.when((t == 4) & (h == 0))
        def _():
            part[:, STEP:HALF] += wide(rq[k, :, 0:128])

    def teacher_peer(k):
        tokens = pl.ds(pl.multiple_of(block_of(k) * 256, 256), 256)
        hq[k] = jnp.transpose(hid[:, tokens])
        rq[k] = across(res[:, tokens], sel).astype(BF16)
        teacher_half(k, peer)
        cs[k] = part[...].astype(BF16)

    loads[2].wait()
    htwo[...] = across(hrow[...], sel)
    hw[1 + t] = htwo[pl.ds(pl.multiple_of(row_block % 2 * 64, 64), 64), :].astype(BF16)

    pl.semaphore_wait(barrier, len(greeted))

    core_id = ids(4)

    def core_copy(k):
        return remote(cs.at[k], cr.at[k], core_id + k, at(c=peer))

    x_id = ids(1)

    def x_copy():
        return remote(xs.at[c], xs.at[c], x_id, at(c=peer))

    loads[3].wait()
    x_copy().start()

    hz_id = ids(3)

    def hz_copy(o):
        return remote(hw.at[1 + t], hw.at[1 + t], hz_id + o - 1, at(p=(p + o) % 4))

    for o in (1, 3, 2):
        hz_copy(o).start()

    hc_id = ids(4)

    def hc_copy(o):
        slot = 1 + 2 * ((p + 4 - o) % 4) + c
        return remote(hw.at[slot], hw.at[slot], hc_id + o, at(c=peer))

    h1_id = ids(6)

    def h1_copy(m, o):
        block = hd.at[x, y, :, pl.ds(896 * m, 896 - 128 * m)]
        device = at(x=(x + o) % 4) if m == 0 else at(y=(y + o) % 4)
        return remote(block, block, h1_id + 3 * m + o - 1, device)

    h2_id = ids(8)

    def h2_copy(m, n):
        a = y if m == 0 else x
        ahead, behind = (a + 1) % 4, (a + 3) % 4
        group = a if n < 2 else behind if n == 2 else ahead
        inner = pl.ds(0, 4) if n < 2 else pl.ds(2 * (n - 2), 2)
        to = ahead if n in (0, 2) else behind
        if m == 0:
            block, device = hd.at[inner, group, :, pl.ds(0, 896)], at(y=to)
        else:
            block, device = hd.at[group, inner, :, pl.ds(896, 768)], at(x=to)
        return remote(block, block, h2_id + 4 * m + n, device)

    def head_first():
        for o in range(4):
            if o:
                hz_copy(o).wait_recv()
            hc_copy(o).start()
        for o in range(4):
            hc_copy(o).wait_recv()
        for j in range(13):
            tile = hw[1 + 4 * c + j // 3, :, (j % 3) * 128 : (j % 3) * 128 + 128]
            if j % 3 == 0:
                tile = tile + hw[4 * c + j // 3, :, 384:512]
            hd[x, y, :, j * 128 : (j + 1) * 128] = tile
        for o in (1, 3, 2):
            for m in range(2):
                h1_copy(m, o).start()

    def head_second():
        for o in range(1, 4):
            for m in range(2):
                h1_copy(m, o).wait_recv()
        for n in range(2):
            for m in range(2):
                h2_copy(m, n).start()

    def head_third():
        for n in range(2):
            for m in range(2):
                h2_copy(m, n).wait_recv()
                h2_copy(m, n + 2).start()

    loads[0].wait()
    loads[1].wait()
    for load in loads[4:]:
        load.wait()
    teacher_peer(0)
    core_copy(0).start()

    a_id, b_id = ids(3 * CH), ids(3 * CH)
    rows = 128 // CH

    def a_copy(slot, piece):
        own = pl.ds(piece * rows, rows)
        src = fa.at[own] if slot == 2 else zs.at[slot, own]
        return remote(src, ra.at[slot, own], a_id + slot * CH + piece, at(p=p1))

    def b_copy(slot, piece):
        own = pl.ds(piece * rows, rows)
        src = fb.at[own] if slot == 2 else zs.at[2 * slot, pl.ds(128 + piece * rows, rows)]
        return remote(src, rb.at[slot, own], b_id + slot * CH + piece, at(p=p3))

    def teacher_step(k, carry):
        teacher_half(k, c)

        core_copy(k).wait_recv()
        zs[k] = (part[...] + wide(cr[k])).astype(BF16)

        @pl.when(k == 0)
        def _():
            for piece in range(CH):
                a_copy(0, piece).start()
                b_copy(0, piece).start()

        @pl.when(k == 1)
        def _():
            for piece in range(CH):
                a_copy(1, piece).start()

        @pl.when(k < 3)
        def _():
            teacher_peer(k + 1)
            core_copy(k + 1).start()

        @pl.when(k == 0)
        def _():
            head_first()

        @pl.when(k == 2)
        def _():
            head_second()

        return carry

    lax.fori_loop(0, 4, teacher_step, 0)

    def normalize(values):
        centered = values - jnp.mean(values, axis=1, keepdims=True)
        inverse = lax.rsqrt(jnp.mean(centered * centered, axis=1, keepdims=True) + epsilon)
        return centered * inverse, inverse

    x_copy().wait_recv()
    for h in range(2):
        normed, _ = normalize(wide(xs[h]))
        out = (normed * gain_ref[...]).astype(BF16)
        nb[h * 128 : (h + 1) * 128, :] = out
        turned = jnp.transpose(wide(out)).astype(BF16)
        nt[:, :, :, :, h * 128 : (h + 1) * 128] = turned.reshape(2, 4, 4, 32, 128)

    def piece_of(piece, first=0):
        return pl.ds(pl.multiple_of(first + piece * rows, rows), rows)

    def second_step(piece, carry):
        own = piece_of(piece)
        a_copy(0, piece).wait_recv()
        fb[own, :] = (wide(zs[2, own, :]) + wide(ra[0, own, :])).astype(BF16)
        b_copy(2, piece).start()
        b_copy(0, piece).wait_recv()
        fa[own, :] = (wide(zs[1, piece_of(piece, 128), :]) + wide(rb[0, own, :])).astype(BF16)
        a_copy(2, piece).start()
        return carry

    lax.fori_loop(0, CH, second_step, 0)
    head_third()
    for piece in range(CH):
        b_copy(1, piece).start()

    for m in range(2):
        for n in (2, 3):
            h2_copy(m, n).wait_recv()
    head = hd[...].reshape(1024, HALF)

    def predict(h, carry):
        block = pl.ds(pl.multiple_of(h * 128, 128), 128)
        pr[block, :] = jnp.dot(nb[block, :], head, preferred_element_type=F32)
        squares[block, :] = jnp.broadcast_to(
            jnp.sum(pr[block, :] * pr[block, :] * mine, axis=1, keepdims=True), (128, 128)
        )
        return carry

    lane = lax.broadcasted_iota(jnp.int32, (1, HALF), 1)
    mine = (lane >= 128 * c).astype(F32)
    small = lax.broadcasted_iota(jnp.int32, (rows, 128), 1)

    stat_id = ids(2 * CH)

    def stat_copy(h, piece):
        own = pl.ds(piece * rows, rows)
        return remote(st.at[h, own], sr.at[h, own], stat_id + h * CH + piece, at(c=peer))

    lax.fori_loop(0, 2, predict, 0)

    def finish(h):
        one, two = (ra, rb) if h == 0 else (rb, ra)

        def sums(piece, carry):
            (a_copy if h == 0 else b_copy)(1, piece).wait_recv()
            (b_copy if h == 0 else a_copy)(2, piece).wait_recv()
            own, block = piece_of(piece), piece_of(piece, h * 128)
            total = wide(zs[3, block, :]) + wide(one[1, own, :]) + wide(two[2, own, :])
            target = total.astype(BF16)
            tg[block, :] = target
            target = wide(target)
            masked = target * mine
            inner = jnp.sum(masked * pr[block, :], axis=1, keepdims=True)
            aim = jnp.sum(masked * target, axis=1, keepdims=True)
            st[h, own, :] = jnp.where(
                small == 0, inner, jnp.where(small == 1, squares[block, :], aim)
            )
            stat_copy(h, piece).start()
            return carry

        def grads(piece, carry):
            own, block = piece_of(piece), piece_of(piece, h * 128)
            stat_copy(h, piece).wait_recv()
            both = st[h, own, :] + sr[h, own, :]
            inner, square, aim = both[:, 0:1], both[:, 1:2], both[:, 2:3]
            scaling = lax.rsqrt((square + epsilon) * (aim + epsilon))
            cosine = inner * scaling
            pg[block, :] = (
                (cosine / (square + epsilon)) * pr[block, :] - scaling * wide(tg[block, :])
            ).astype(BF16)
            losses[own, :] = jnp.broadcast_to(1.0 - cosine, (rows, 128))
            return carry

        lax.fori_loop(0, CH, sums, 0)
        lax.fori_loop(0, CH, grads, 0)

        @pl.when(c == h)
        def _():
            loss_ref[...] = jnp.transpose(losses[...])[0:1, :]

    def back(h):
        grad = pg[h * 128 : (h + 1) * 128, :] * mine.astype(BF16)

        def one(q, carry):
            bp[h, :, pl.ds(pl.multiple_of(q * 256, 256), 256)] = lax.dot_general(
                grad, hd[q].reshape(256, HALF), (((1,), (1,)), ((), ())),
                preferred_element_type=F32,
            )
            return carry

        lax.fori_loop(0, 4, one, 0)

    finish(0)
    back(0)
    finish(1)

    parts = (pl.ds(0, 896), pl.ds(896, 768))
    gs, r1, f1, s1, r2 = (gs0, gs1), (r10, r11), (f10, f11), (s10, s11), (r20, r21)
    g_id = ids(24)
    axes = []
    for m in range(2):
        a = x if m == 0 else y
        axes.append((a, a + 1 - 2 * (a % 2), (a + 2) % 4, 3 - a))

    def g_copy(n, m, way, slot):
        a, near, far, last = axes[m]
        to = near if way == 0 else last
        device = at(x=to) if m == 0 else at(y=to)
        if slot == 2:
            src = f1[n].at[m, way]
        else:
            src = gs[n].at[m, far if slot == 0 else to, pl.ds(2 * way, 2)]
        dst = r1[n].at[m, way, slot]
        return remote(src, dst, g_id + n * 12 + m * 6 + way * 3 + slot, device)

    def gradient(n, send):
        def turn(j, carry):
            ax, ay = [
                jnp.where(j == 0, far, jnp.where(j == 1, near, jnp.where(j == 2, last, a)))
                for a, near, far, last in axes
            ]
            left = jnp.concatenate(
                [nt[0, ax].reshape(128, 256), nt[1, :, ay].reshape(128, 256)], axis=0
            )
            both = jnp.dot(left, pg[:, parts[n]], preferred_element_type=F32).astype(BF16)
            gs[n][0, ax] = both[0:128].reshape(4, 32, -1)
            gs[n][1, ay] = both[128:256].reshape(4, 32, -1)
            if send:

                @pl.when(j == 0)
                def _():
                    first_sends(n, 0)

                @pl.when(j == 2)
                def _():
                    first_sends(n, 1)

            return carry

        lax.fori_loop(0, 4, turn, 0)

    def first_sends(n, slot):
        for m in range(2):
            for way in range(2):
                g_copy(n, m, way, slot).start()

    def forward(n):
        for m in range(2):
            a, near, far, last = axes[m]
            for way in range(2):
                g_copy(n, m, 1 - way, 0).wait_recv()
                target, inner = (near, slice(2, 4)) if way == 0 else (last, slice(0, 2))
                f1[n][m, way] = (
                    wide(gs[n][m, target, inner])
                    + wide(r1[n][m, 1 - way, 0])
                ).astype(BF16)
                g_copy(n, m, way, 2).start()

    g2_id = ids(12)

    def g2_copy(n, m, o):
        b = y if m == 0 else x
        to = (b + o) % 4
        device = at(y=to) if m == 0 else at(x=to)
        return remote(
            s1[n].at[m, to], r2[n].at[m, o - 1],
            g2_id + 6 * n + 3 * m + o - 1, device,
        )

    def second_sends(n):
        for m in range(2):
            a = axes[m][0]
            for slot in (1, 2):
                for way in range(2):
                    g_copy(n, m, way, slot).wait_recv()
            for way in range(2):
                inner = slice(2 * way, 2 * way + 2)
                s1[n][m, inner] = (
                    wide(gs[n][m, a, inner])
                    + wide(r1[n][m, way, 1])
                    + wide(r1[n][m, 1 - way, 2])
                ).astype(BF16)
            for o in (1, 3, 2):
                g2_copy(n, m, o).start()

    def second_sums(n):
        for m in range(2):
            total = wide(s1[n][m, axes[1 - m][0]])
            for o in range(1, 4):
                g2_copy(n, m, o).wait_recv()
                total = total + wide(r2[n][m, o - 1])
            s2[m, :, parts[n]] = total.astype(BF16)

    g3_id = ids(16)

    def window_of(chip, core):
        return pl.ds(pl.multiple_of(768 * (chip % 2) + 384 * core, 128), WIDE)

    def g3_copy(o, core):
        to = (zz + o) % 8
        src = s2.at[to % 2, :, window_of(to // 2, core)]
        return remote(src, rz.at[o], g3_id + 2 * o + core, at(zl=to % 2, p=to // 2, c=core))

    def third(n, act):
        for o in (0, 1, 7, 2, 6, 3, 5, 4):
            chip = ((zz + o) % 8) // 2

            @pl.when((chip // 2 == c) & (chip % 2 == n))
            def _():
                if o:
                    act(g3_copy(o, c))
                act(g3_copy(o, peer))

    def third_sends(n):
        third(n, lambda copy: copy.start())

    gradient(0, True)
    gradient(1, False)
    forward(0)
    first_sends(1, 0)
    first_sends(1, 1)

    back(1)
    back_id = ids(1)

    def back_copy():
        return remote(bp.at[peer], br, back_id, at(c=peer))

    back_copy().start()
    second_sends(0)
    forward(1)

    second_sums(0)
    third_sends(0)
    second_sends(1)
    second_sums(1)
    third_sends(1)

    back_copy().wait_recv()
    normed, inverse = normalize(wide(xs[c]))
    normed_grad = (bp[c] + br[...]) * gain_ref[...]
    igrad_ref[...] = (
        inverse
        * (
            normed_grad
            - jnp.mean(normed_grad, axis=1, keepdims=True)
            - normed * jnp.mean(normed_grad * normed, axis=1, keepdims=True)
        )
    ).astype(BF16)

    @pl.when(p // 2 == c)
    def _():
        rz[0] = s2[zl, :, window_of(p, c)]

    @pl.when(p // 2 != c)
    def _():
        g3_copy(0, c).wait_recv()

    total = wide(rz[0])
    for o in range(1, 8):
        g3_copy(o, c).wait_recv()
        total = total + wide(rz[o])
    hgrad_ref[...] = total.astype(BF16)

    x_copy().wait_send()
    for o in range(1, 4):
        hz_copy(o).wait_send()
        for m in range(2):
            h1_copy(m, o).wait_send()
            for n in range(2):
                g2_copy(n, m, o).wait_send()
    for o in range(4):
        hc_copy(o).wait_send()
        for m in range(2):
            h2_copy(m, o).wait_send()
        core_copy(o).wait_send()
    for slot in range(3):
        for piece in range(CH):
            a_copy(slot, piece).wait_send()
            b_copy(slot, piece).wait_send()
        for m in range(2):
            for way in range(2):
                for n in range(2):
                    g_copy(n, m, way, slot).wait_send()
    for h in range(2):
        for piece in range(CH):
            stat_copy(h, piece).wait_send()
    back_copy().wait_send()
    for n in range(2):
        third(n, lambda copy: copy.wait_send())


def place(loss_ref, igrad_ref, hgrad_ref, loss_out, igrad_out, hgrad_out):
    loss_out[...] = loss_ref[...]
    igrad_out[...] = igrad_ref[...]
    t = lax.axis_index("tensor")
    first = 32 * (t // 2) + 16 * (t % 2)
    row = lax.broadcasted_iota(jnp.int32, (WIDE, 400), 0)
    pick = (row == lax.broadcasted_iota(jnp.int32, (WIDE, 400), 1) + first).astype(BF16)
    hgrad_out[...] = jnp.dot(hgrad_ref[...], pick, preferred_element_type=F32).astype(BF16)


def shards(
    teacher_hidden, down_weight, teacher_resid, layer_scale, student_x, norm_gain, head_weight
):
    hbm = pl.BlockSpec(memory_space=pl.ANY)
    vmem = pl.BlockSpec(memory_space=pltpu.VMEM)
    scratch = [
        ((800, 1024), BF16),
        ((4, 256, 800), BF16),
        ((4, 256, WIDE), BF16),
        ((800, DT), BF16),
        ((400, 1024), BF16),
        ((400, 128), BF16),
        ((128, WIDE), F32),
        ((1, DT), F32),
        ((256, HALF), F32),
        ((4, 256, HALF), BF16),
        ((4, 256, HALF), BF16),
        ((4, 256, HALF), BF16),
        ((3, 128, HALF), BF16),
        ((3, 128, HALF), BF16),
        ((128, HALF), BF16),
        ((128, HALF), BF16),
        ((10, 64, WIDE), BF16),
        ((4, 4, 64, HALF), BF16),
        ((2, 128, 1024), BF16),
        ((256, 1024), BF16),
        ((2, 4, 4, 32, 256), BF16),
        ((256, HALF), F32),
        ((256, HALF), BF16),
        ((256, 128), F32),
        ((256, HALF), BF16),
        ((128, 128), F32),
        ((2, 128, 128), F32),
        ((2, 128, 128), F32),
        ((2, 128, 1024), F32),
        ((128, 1024), F32),
        ((2, 4, 4, 32, 896), BF16),
        ((2, 4, 4, 32, 768), BF16),
        ((2, 2, 3, 2, 32, 896), BF16),
        ((2, 2, 3, 2, 32, 768), BF16),
        ((2, 2, 2, 32, 896), BF16),
        ((2, 2, 2, 32, 768), BF16),
        ((2, 4, 32, 896), BF16),
        ((2, 4, 32, 768), BF16),
        ((2, 3, 32, 896), BF16),
        ((2, 3, 32, 768), BF16),
        ((2, 32, HALF), BF16),
        ((8, 32, WIDE), BF16),
    ]
    copies = 1 + 3 + 4 + 6 + 8 + 4 + 6 * CH + 2 * CH + 24 + 12 + 16 + 1
    loss, input_grad, head_grad = pl.pallas_call(
        kernel,
        name="distill",
        out_shape=(
            jax.ShapeDtypeStruct((1, 128), F32),
            jax.ShapeDtypeStruct((128, 1024), BF16),
            jax.ShapeDtypeStruct((32, WIDE), BF16),
        ),
        in_specs=[hbm, hbm, hbm, vmem, hbm, vmem, hbm],
        out_specs=(vmem, vmem, vmem),
        scratch_shapes=[pltpu.VMEM(shape, kind) for shape, kind in scratch]
        + [
            pltpu.SemaphoreType.DMA((8,)),
            pltpu.SemaphoreType.DMA((copies,)),
            pltpu.SemaphoreType.DMA((copies,)),
        ],
        compiler_params=pltpu.CompilerParams(
            collective_id=0, has_side_effects=True, vmem_limit_bytes=60 * 2**20
        ),
        cost_estimate=pl.CostEstimate(
            flops=8_000_000_000, bytes_accessed=10_000_000, transcendentals=1000
        ),
    )(
        teacher_hidden.T,
        down_weight,
        teacher_resid.T,
        layer_scale.reshape(25, 128),
        student_x,
        norm_gain.reshape(1, -1),
        head_weight.T,
    )
    loss, input_grad, head_grad = pl.pallas_call(
        place,
        name="place",
        out_shape=(
            jax.ShapeDtypeStruct((1, 128), F32),
            jax.ShapeDtypeStruct((128, 1024), BF16),
            jax.ShapeDtypeStruct((32, 400), BF16),
        ),
        in_specs=[vmem, vmem, vmem],
        out_specs=(vmem, vmem, vmem),
    )(loss, input_grad, head_grad)
    return (loss.reshape(-1), input_grad, head_grad)


def solution(mesh):
    placed = (
        P("dp", "tensor"),
        P("tensor", None),
        P("dp", "tensor"),
        P(),
        P(("dp", "tensor"), None),
        P(),
        P(None, "tensor"),
    )
    return jax.shard_map(
        shards,
        mesh=mesh,
        in_specs=placed,
        out_specs=(P(("dp", "tensor")), P(("dp", "tensor"), None), P("dp", "tensor")),
        check_vma=False,
    )
```

time: 111 us -> 110 us (level)
  no operation moved by 1% of the time
where the time goes in v4:
time: 110 us
  Pallas kernels  109 us (99%)
    pallas_call x1, Pallas kernels, shards(): pl.pallas_call(kernel, name='distill', out_shape=(jax.ShapeDtypeStruct((1...  107 us

profile of v4, /device:TPU:64, one launch (start us, length us, event | category | flops | bytes accessed | tf_op | source)
XLA Modules:
  0.0 109.9 jit_solution(3434760547222559015)
XLA Ops:
  0.6 107.4 %distill.1 = (f32[1,128]{1,0:T(1,128)}, bf16[128,1024]{1,0:T(8,128)(2,1)}, bf16[32,512]{1,0:T(8,128)(2,1)}) custom-call(bf16[800,1024]{1,0:T(8,128)(2,1)} %bitcast.6, bf16[800,3200]{1,0:T(8,128)(2,1)} %w_hbm.1, bf16[400,1024]{1,0:T(8,128)(2,1)} %bitcast.7, f32[25,128]{1,0:T(8,128)} %bitcast.9, bf16[128,1024]{1,0:T(8,128)(2,1)} %x_hbm.1, f32[1,1024]{1,0:T(1,128)} %bitcast.10, ...), custom_call_target="tpu_custom_call" | custom-call | flops 8000000000 | bytes 10000000 | tf_op jit(solution)/shard_map/distill/pallas_call | solution.py:631
  108.1 1.8 %place.1 = (f32[1,128]{1,0:T(1,128)}, bf16[128,1024]{1,0:T(8,128)(2,1)}, bf16[32,400]{1,0:T(8,128)(2,1)}) custom-call(f32[1,128]{1,0:T(1,128)} %get-tuple-element.9.loss_ref, bf16[128,1024]{1,0:T(8,128)(2,1)} %get-tuple-element.10.igrad_ref, bf16[32,512]{1,0:T(8,128)(2,1)} %get-tuple-element.11.hgrad_ref), custom_call_target="tpu_custom_call" | custom-call | tf_op jit(solution)/shard_map/place/pallas_call | solution.py:662
